TPU v7x, 128 devices: a whole 4x4x4 slice. The times are simulated.
128 devices in a mesh: ctx: 32 (over z, y, core), head: 4 (over x).
Axes of the slice: x: 4, y: 4, z: 4, core: 2. Of those that a mesh axis runs over, the one named last changes fastest.
Arguments:
- query: bfloat16 [8192, 8192], P('ctx', 'head'), may hold values from -5 to 5
- keys: bfloat16 [8192, 1024], P('ctx', 'head'), may hold values from -5 to 5
- values: bfloat16 [8192, 1024], P('ctx', 'head'), may hold values from -6 to 6
- out_saved: bfloat16 [8192, 8192], P('ctx', 'head'), may hold values from -4 to 4
- d_out: bfloat16 [8192, 8192], P('ctx', 'head'), may hold values from -6 to 6
- doc_ids: int32 [8192], P(('ctx', 'head')), may hold values from 0 to 4, as said below
- placement: int32 [32], replicated, may hold values from 0 to 31, as said below
- block_keys: int32 [32, 12], replicated, may hold values from 0 to 31, as said below
Outputs:
- grad_query: bfloat16 [8192, 8192], P('ctx', 'head')
- grad_keys: bfloat16 [8192, 1024], P('ctx', 'head')
- grad_values: bfloat16 [8192, 1024], P('ctx', 'head')
Inputs may be any that keep to these rules, and one draw needn't show every extreme that they name: `placement`: A permutation of the block positions. `doc_ids`: read in packed-sequence order (block placement[s] holds stored block s), ids start at 0, never fall, and rise by one at exactly 4 positions. `block_keys`: column 0 of row b is b; every other entry of row b lies between b - 24 and b; entries may repeat.
All inputs are finite; a program needn't handle non-finite values.
Results may differ from a plain program's by a relative error of at most 0.014.
Values may be sent and summed in bfloat16 or wider, within the bound.
No kernel may reach another device: no remote copies, remote signals or barrier semaphores. Data moves between devices by JAX's collectives and lax.ppermute only.
A program may use at most 128 MiB of HBM per device.

v0:
```python
import math

import jax
import jax.numpy as jnp
from jax import lax
from jax.sharding import PartitionSpec as P

HD = 128
BLOCK = 256


neg_big = -1e30


def tile_table(placement, block_keys, device, blocks_here):
    count = placement.shape[0]
    slots = jnp.arange(count, dtype=jnp.int32)
    owner_list, slot_list, first_list, query_pos = ([], [], [], [])
    slot_here = device * blocks_here + 0
    global_block = jnp.sum(jnp.where(slots == slot_here, placement, 0))
    chosen = lax.dynamic_slice_in_dim(block_keys, global_block, 1, 0)[0]
    same = chosen[:, None] == chosen[None, :]
    first_list.append(jnp.logical_not(jnp.any(jnp.tril(same, -1), axis=1)))
    slot_list.append(
        jnp.sum(jnp.where(placement[None, :] == chosen[:, None], slots[None, :], 0), axis=1)
    )
    owner_list.append(jnp.full((chosen.shape[0],), 0, jnp.int32))
    query_pos.append(global_block * BLOCK + jnp.arange(BLOCK, dtype=jnp.int32))
    return (owner_list[0], slot_list[0], first_list[0], jnp.stack(query_pos))


def pad_rows(array):
    margin = jnp.zeros((BLOCK,) + array.shape[1:], array.dtype)
    return jnp.concatenate([margin, array, margin], axis=0)


def shards(query, keys, values, out_saved, d_out, doc_ids, placement, block_keys):
    own_docs = lax.all_gather(doc_ids, "head", axis=0, tiled=True)
    scale = 1.0 / math.sqrt(HD)
    row_count = query.shape[0]
    blocks_here = row_count // BLOCK
    kv_local = keys.shape[1] // HD
    group = query.shape[1] // keys.shape[1]
    all_rows = placement.shape[0] * BLOCK
    device = lax.axis_index("ctx")
    owners, key_slots, firsts, query_pos = tile_table(placement, block_keys, device, blocks_here)
    tiles = owners.shape[0]
    key_pos_all = (
        placement[:, None] * BLOCK + jnp.arange(BLOCK, dtype=jnp.int32)[None, :]
    ).reshape(-1)
    query_four = query.reshape(blocks_here, BLOCK, kv_local, group, HD)
    grads_four = d_out.reshape(blocks_here, BLOCK, kv_local, group, HD)
    saved_four = out_saved.reshape(blocks_here, BLOCK, kv_local, group, HD)
    delta = jnp.einsum(
        "bighd,bighd->bghi", grads_four, saved_four, preferred_element_type=jnp.float32
    )
    query_docs = own_docs.reshape(blocks_here, BLOCK)

    def intersections(tile_index, length):
        offset = key_slots[tile_index] * BLOCK
        return (offset < length) & (offset + BLOCK > 0)

    def prepare(tile_index, padded, length):
        padded_keys, padded_values, padded_docs = padded
        local = owners[tile_index]
        slot_here = key_slots[tile_index]
        offset = slot_here * BLOCK
        offsets = offset + jnp.arange(BLOCK, dtype=jnp.int32)
        inside = (offsets >= 0) & (offsets < length)
        begin = jnp.clip(offset + BLOCK, 0, length + BLOCK)
        key_tile = lax.dynamic_slice_in_dim(padded_keys, begin, BLOCK, 0).reshape(
            BLOCK, kv_local, HD
        )
        value_tile = lax.dynamic_slice_in_dim(padded_values, begin, BLOCK, 0).reshape(
            BLOCK, kv_local, HD
        )
        key_docs = lax.dynamic_slice_in_dim(padded_docs, begin, BLOCK, 0)
        key_pos = lax.dynamic_slice_in_dim(key_pos_all, slot_here * BLOCK, BLOCK)
        visible = inside[None, :] & (query_docs[local][:, None] == key_docs[None, :])
        visible = visible & (key_pos[None, :] <= query_pos[local][:, None]) & firsts[tile_index]
        scores = (
            jnp.einsum(
                "ighd,jgd->ghij", query_four[local], key_tile, preferred_element_type=jnp.float32
            )
            * scale
        )
        return (local, slot_here, key_tile, value_tile, visible, scores)

    stat_start = (
        jnp.full((blocks_here, kv_local, group, BLOCK), neg_big, jnp.float32),
        jnp.zeros((blocks_here, kv_local, group, BLOCK), jnp.float32),
    )
    grad_start = (
        jnp.zeros((blocks_here, BLOCK, kv_local, group, HD), jnp.float32),
        jnp.zeros((all_rows, kv_local * HD), jnp.float32),
        jnp.zeros((all_rows, kv_local * HD), jnp.float32),
    )
    pieces = (
        lax.all_gather(keys, "ctx", axis=0, tiled=True),
        lax.all_gather(values, "ctx", axis=0, tiled=True),
        lax.all_gather(own_docs, "ctx", axis=0, tiled=True),
    )
    length = pieces[0].shape[0]
    padded = (pad_rows(pieces[0]), pad_rows(pieces[1]), pad_rows(pieces[2]))

    def add_tile_step(tile_index, state):

        def add_compute(state):
            running_max, running_sum = state
            local, slot_here, key_tile, value_tile, visible, scores = prepare(
                tile_index, padded, length
            )
            masked = jnp.where(visible, scores, neg_big)
            old_max = running_max[local]
            new_max = jnp.maximum(old_max, jnp.max(masked, axis=-1))
            weights = jnp.where(visible, jnp.exp(scores - new_max[..., None]), 0.0)
            fresh = running_sum[local] * jnp.exp(old_max - new_max) + jnp.sum(weights, axis=-1)
            return (running_max.at[local].set(new_max), running_sum.at[local].set(fresh))

        return lax.cond(intersections(tile_index, length), add_compute, lambda kept: kept, state)

    running_max, running_sum = lax.fori_loop(0, tiles, add_tile_step, stat_start)
    log_total = running_max + jnp.log(running_sum)
    pieces = (
        lax.all_gather(keys, "ctx", axis=0, tiled=True),
        lax.all_gather(values, "ctx", axis=0, tiled=True),
        lax.all_gather(own_docs, "ctx", axis=0, tiled=True),
    )
    make_length = pieces[0].shape[0]
    make_padded = (pad_rows(pieces[0]), pad_rows(pieces[1]), pad_rows(pieces[2]))

    def make_tile_step(tile_index, state):

        def make_compute(state):
            query_acc, key_acc, value_acc = state
            local, slot_here, key_tile, value_tile, visible, scores = prepare(
                tile_index, make_padded, make_length
            )
            probs = jnp.where(visible, jnp.exp(scores - log_total[local][..., None]), 0.0).astype(
                jnp.bfloat16
            )
            grad_probs = jnp.einsum(
                "ighd,jgd->ghij", grads_four[local], value_tile, preferred_element_type=jnp.float32
            )
            grad_scores = (
                probs.astype(jnp.float32) * (grad_probs - delta[local][..., None])
            ).astype(jnp.bfloat16)
            query_tile = (
                jnp.einsum(
                    "ghij,jgd->ighd", grad_scores, key_tile, preferred_element_type=jnp.float32
                )
                * scale
            )
            key_grad = (
                jnp.einsum(
                    "ghij,ighd->jgd",
                    grad_scores,
                    query_four[local],
                    preferred_element_type=jnp.float32,
                )
                * scale
            )
            value_grad = jnp.einsum(
                "ghij,ighd->jgd", probs, grads_four[local], preferred_element_type=jnp.float32
            )
            query_acc = query_acc.at[local].add(query_tile)
            begin = slot_here * BLOCK
            old_keys = lax.dynamic_slice_in_dim(key_acc, begin, BLOCK, 0)
            key_acc = lax.dynamic_update_slice_in_dim(
                key_acc, old_keys + key_grad.reshape(BLOCK, -1), begin, 0
            )
            old_values = lax.dynamic_slice_in_dim(value_acc, begin, BLOCK, 0)
            value_acc = lax.dynamic_update_slice_in_dim(
                value_acc, old_values + value_grad.reshape(BLOCK, -1), begin, 0
            )
            return (query_acc, key_acc, value_acc)

        return lax.cond(
            intersections(tile_index, make_length), make_compute, lambda kept: kept, state
        )

    query_acc, key_acc, value_acc = lax.fori_loop(0, tiles, make_tile_step, grad_start)
    key_share, value_share = (
        lax.psum_scatter(
            key_acc.astype(jnp.bfloat16), "ctx", scatter_dimension=0, tiled=True
        ).astype(jnp.float32),
        lax.psum_scatter(
            value_acc.astype(jnp.bfloat16), "ctx", scatter_dimension=0, tiled=True
        ).astype(jnp.float32),
    )
    grad_query = query_acc.reshape(row_count, -1).astype(jnp.bfloat16)
    return (grad_query, key_share.astype(jnp.bfloat16), value_share.astype(jnp.bfloat16))


def solution(mesh):
    placed = (
        P("ctx", "head"),
        P("ctx", "head"),
        P("ctx", "head"),
        P("ctx", "head"),
        P("ctx", "head"),
        P(("ctx", "head")),
        P(),
        P(),
    )
    return jax.shard_map(
        shards,
        mesh=mesh,
        in_specs=placed,
        out_specs=(P("ctx", "head"), P("ctx", "head"), P("ctx", "head")),
        check_vma=False,
    )
```

profile of v0, /device:TPU:0, one launch (start us, length us, event | category | flops | bytes accessed | tf_op | source)
XLA Modules:
  0.0 564.8 jit_solution(13084503780165974888)
XLA Ops:
  15.1 2.5 copy.101
  24.2 9.0 %all-reduce = s32[256]{0:T(256)S(1)} all-reduce(s32[256]{0:T(256)S(1)} %dynamic-update-slice.6), channel_id=1, replica_groups=mesh['ctx'=32,'head'=4] {'head'}, use_global_device_ids=true, to_apply=%add | all-reduce | flops 256 | bytes 2048
  33.2 25.6 %all-gather = s32[32,1,256]{2,1,0:T(1,128)S(1)} all-gather(s32[1,1,256]{2,1,0:T(1,128)S(1)} %bitcast.138), channel_id=1, replica_groups=mesh['ctx'=32,'head'=4] {'ctx'}, dimensions={0}, use_global_device_ids=true | all-gather | bytes 33792 | tf_op jit(solution)/shard_map/all_gather | solution.py:127
  59.0 3.7 all-gather.4.cloned.1.call-done
  62.7 51.6 %all-gather.6.cloned.1.call-done = bf16[8192,256]{0,1:T(8,128)(2,1)} async-done(((bf16[256,256]{0,1:T(8,128)(2,1)}), bf16[8192,256]{0,1:T(8,128)(2,1)}) %all-gather.6.cloned.1.call-update) | async-done | bytes 4194320 | tf_op jit(solution)/shard_map/all_gather | solution.py:126
  114.3 6.0 %pad_maximum_fusion = (bf16[8704,256]{0,1:T(8,128)(2,1)}, bf16[8704,256]{0,1:T(8,128)(2,1)}) fusion(bf16[256,256]{0,1:T(8,128)(2,1)S(1)} %broadcast.168, bf16[8192,256]{0,1:T(8,128)(2,1)} %all-gather.6.cloned.1.call-done, bf16[8192,256]{0,1:T(8,128)(2,1)} %all-gather.4.cloned.1.call-done), kind=kLoop, calls=%fused_computation.40 | loop fusion | flops 22282240 | bytes 17432576 | tf_op jit(solution)/shard_map/concatenate | solution.py:34
  120.3 88.9 %while.37 = (s32[]{:T(128)}, f32[1,2,8,256]{3,2,1,0:T(8,128)S(1)}, f32[1,2,8,256]{3,2,1,0:T(8,128)S(1)}, s32[12]{0:T(128)S(1)}, s32[256]{0:T(256)S(1)}, /*index=...) while((s32[]{:T(128)}, f32[1,2,8,256]{3,2,1,0:T(8,128)S(1)}, ...), condition=%wide.region_8.9_spmd.clone, body=%wide.region_3.8_spmd.clone.sunk | while | flops 276124928 | bytes 12497022 | solution.py:122
  121.6 6.1 %conditional.6 = ((f32[1,2,8,256]{3,2,1,0:T(8,128)S(1)}, f32[1,2,8,256]{3,2,1,0:T(8,128)S(1)})) conditional(s32[]{:T(128)} %bitcast.117, (f32[1,2,8,256]{3,2,1,0:T(8,128)S(1)}, f32[1,2,8,256]{3,2,1,0:T(8,128)S(1)}) %tuple.103, (s32[]{:T(128)}, s32[12]{0:T(128)S(1)}, s32[256]{0:T(256)S(1)}, s32[8704]{0:T(1024)S(1)}, s32[32]{0:T(128)S(1)}, ...), branch_computations={%region_4.4_spmd, %region_5.7_spmd} | conditional | flops 276124928 | bytes 12462899 | solution.py:120
  129.0 6.1 %conditional.6 = ((f32[1,2,8,256]{3,2,1,0:T(8,128)S(1)}, f32[1,2,8,256]{3,2,1,0:T(8,128)S(1)})) conditional(s32[]{:T(128)} %bitcast.117, (f32[1,2,8,256]{3,2,1,0:T(8,128)S(1)}, f32[1,2,8,256]{3,2,1,0:T(8,128)S(1)}) %tuple.103, (s32[]{:T(128)}, s32[12]{0:T(128)S(1)}, s32[256]{0:T(256)S(1)}, s32[8704]{0:T(1024)S(1)}, s32[32]{0:T(128)S(1)}, ...), branch_computations={%region_4.4_spmd, %region_5.7_spmd} | conditional | flops 276124928 | bytes 12462899 | solution.py:120
  136.4 6.1 %conditional.6 = ((f32[1,2,8,256]{3,2,1,0:T(8,128)S(1)}, f32[1,2,8,256]{3,2,1,0:T(8,128)S(1)})) conditional(s32[]{:T(128)} %bitcast.117, (f32[1,2,8,256]{3,2,1,0:T(8,128)S(1)}, f32[1,2,8,256]{3,2,1,0:T(8,128)S(1)}) %tuple.103, (s32[]{:T(128)}, s32[12]{0:T(128)S(1)}, s32[256]{0:T(256)S(1)}, s32[8704]{0:T(1024)S(1)}, s32[32]{0:T(128)S(1)}, ...), branch_computations={%region_4.4_spmd, %region_5.7_spmd} | conditional | flops 276124928 | bytes 12462899 | solution.py:120
  143.8 6.1 %conditional.6 = ((f32[1,2,8,256]{3,2,1,0:T(8,128)S(1)}, f32[1,2,8,256]{3,2,1,0:T(8,128)S(1)})) conditional(s32[]{:T(128)} %bitcast.117, (f32[1,2,8,256]{3,2,1,0:T(8,128)S(1)}, f32[1,2,8,256]{3,2,1,0:T(8,128)S(1)}) %tuple.103, (s32[]{:T(128)}, s32[12]{0:T(128)S(1)}, s32[256]{0:T(256)S(1)}, s32[8704]{0:T(1024)S(1)}, s32[32]{0:T(128)S(1)}, ...), branch_computations={%region_4.4_spmd, %region_5.7_spmd} | conditional | flops 276124928 | bytes 12462899 | solution.py:120
  151.2 6.1 %conditional.6 = ((f32[1,2,8,256]{3,2,1,0:T(8,128)S(1)}, f32[1,2,8,256]{3,2,1,0:T(8,128)S(1)})) conditional(s32[]{:T(128)} %bitcast.117, (f32[1,2,8,256]{3,2,1,0:T(8,128)S(1)}, f32[1,2,8,256]{3,2,1,0:T(8,128)S(1)}) %tuple.103, (s32[]{:T(128)}, s32[12]{0:T(128)S(1)}, s32[256]{0:T(256)S(1)}, s32[8704]{0:T(1024)S(1)}, s32[32]{0:T(128)S(1)}, ...), branch_computations={%region_4.4_spmd, %region_5.7_spmd} | conditional | flops 276124928 | bytes 12462899 | solution.py:120
  158.6 6.1 %conditional.6 = ((f32[1,2,8,256]{3,2,1,0:T(8,128)S(1)}, f32[1,2,8,256]{3,2,1,0:T(8,128)S(1)})) conditional(s32[]{:T(128)} %bitcast.117, (f32[1,2,8,256]{3,2,1,0:T(8,128)S(1)}, f32[1,2,8,256]{3,2,1,0:T(8,128)S(1)}) %tuple.103, (s32[]{:T(128)}, s32[12]{0:T(128)S(1)}, s32[256]{0:T(256)S(1)}, s32[8704]{0:T(1024)S(1)}, s32[32]{0:T(128)S(1)}, ...), branch_computations={%region_4.4_spmd, %region_5.7_spmd} | conditional | flops 276124928 | bytes 12462899 | solution.py:120
  166.1 6.1 %conditional.6 = ((f32[1,2,8,256]{3,2,1,0:T(8,128)S(1)}, f32[1,2,8,256]{3,2,1,0:T(8,128)S(1)})) conditional(s32[]{:T(128)} %bitcast.117, (f32[1,2,8,256]{3,2,1,0:T(8,128)S(1)}, f32[1,2,8,256]{3,2,1,0:T(8,128)S(1)}) %tuple.103, (s32[]{:T(128)}, s32[12]{0:T(128)S(1)}, s32[256]{0:T(256)S(1)}, s32[8704]{0:T(1024)S(1)}, s32[32]{0:T(128)S(1)}, ...), branch_computations={%region_4.4_spmd, %region_5.7_spmd} | conditional | flops 276124928 | bytes 12462899 | solution.py:120
  173.5 6.1 %conditional.6 = ((f32[1,2,8,256]{3,2,1,0:T(8,128)S(1)}, f32[1,2,8,256]{3,2,1,0:T(8,128)S(1)})) conditional(s32[]{:T(128)} %bitcast.117, (f32[1,2,8,256]{3,2,1,0:T(8,128)S(1)}, f32[1,2,8,256]{3,2,1,0:T(8,128)S(1)}) %tuple.103, (s32[]{:T(128)}, s32[12]{0:T(128)S(1)}, s32[256]{0:T(256)S(1)}, s32[8704]{0:T(1024)S(1)}, s32[32]{0:T(128)S(1)}, ...), branch_computations={%region_4.4_spmd, %region_5.7_spmd} | conditional | flops 276124928 | bytes 12462899 | solution.py:120
  180.9 6.1 %conditional.6 = ((f32[1,2,8,256]{3,2,1,0:T(8,128)S(1)}, f32[1,2,8,256]{3,2,1,0:T(8,128)S(1)})) conditional(s32[]{:T(128)} %bitcast.117, (f32[1,2,8,256]{3,2,1,0:T(8,128)S(1)}, f32[1,2,8,256]{3,2,1,0:T(8,128)S(1)}) %tuple.103, (s32[]{:T(128)}, s32[12]{0:T(128)S(1)}, s32[256]{0:T(256)S(1)}, s32[8704]{0:T(1024)S(1)}, s32[32]{0:T(128)S(1)}, ...), branch_computations={%region_4.4_spmd, %region_5.7_spmd} | conditional | flops 276124928 | bytes 12462899 | solution.py:120
  188.3 6.1 %conditional.6 = ((f32[1,2,8,256]{3,2,1,0:T(8,128)S(1)}, f32[1,2,8,256]{3,2,1,0:T(8,128)S(1)})) conditional(s32[]{:T(128)} %bitcast.117, (f32[1,2,8,256]{3,2,1,0:T(8,128)S(1)}, f32[1,2,8,256]{3,2,1,0:T(8,128)S(1)}) %tuple.103, (s32[]{:T(128)}, s32[12]{0:T(128)S(1)}, s32[256]{0:T(256)S(1)}, s32[8704]{0:T(1024)S(1)}, s32[32]{0:T(128)S(1)}, ...), branch_computations={%region_4.4_spmd, %region_5.7_spmd} | conditional | flops 276124928 | bytes 12462899 | solution.py:120
  195.7 6.1 %conditional.6 = ((f32[1,2,8,256]{3,2,1,0:T(8,128)S(1)}, f32[1,2,8,256]{3,2,1,0:T(8,128)S(1)})) conditional(s32[]{:T(128)} %bitcast.117, (f32[1,2,8,256]{3,2,1,0:T(8,128)S(1)}, f32[1,2,8,256]{3,2,1,0:T(8,128)S(1)}) %tuple.103, (s32[]{:T(128)}, s32[12]{0:T(128)S(1)}, s32[256]{0:T(256)S(1)}, s32[8704]{0:T(1024)S(1)}, s32[32]{0:T(128)S(1)}, ...), branch_computations={%region_4.4_spmd, %region_5.7_spmd} | conditional | flops 276124928 | bytes 12462899 | solution.py:120
  203.1 6.1 %conditional.6 = ((f32[1,2,8,256]{3,2,1,0:T(8,128)S(1)}, f32[1,2,8,256]{3,2,1,0:T(8,128)S(1)})) conditional(s32[]{:T(128)} %bitcast.117, (f32[1,2,8,256]{3,2,1,0:T(8,128)S(1)}, f32[1,2,8,256]{3,2,1,0:T(8,128)S(1)}) %tuple.103, (s32[]{:T(128)}, s32[12]{0:T(128)S(1)}, s32[256]{0:T(256)S(1)}, s32[8704]{0:T(1024)S(1)}, s32[32]{0:T(128)S(1)}, ...), branch_computations={%region_4.4_spmd, %region_5.7_spmd} | conditional | flops 276124928 | bytes 12462899 | solution.py:120
  209.5 4.2 broadcast.167.clone
  213.7 4.2 broadcast.167
  217.9 165.7 %while.38 = (s32[]{:T(128)}, f32[1,256,2,8,128]{1,4,3,2,0:T(8,128)S(1)}, f32[8192,256]{0,1:T(8,128)}, f32[8192,256]{0,1:T(8,128)}, s32[12]{0:T(128)S(1)}, /*inde...) while((s32[]{:T(128)}, ...), condition=%wide.region_12.13_spmd.clone, body=%wide.region_9.12_spmd.clone.sunk | while | flops 1352148224 | bytes 28520708 | solution.py:182
  219.1 12.6 %conditional.7 = ((f32[1,256,2,8,128]{1,4,3,2,0:T(8,128)S(1)}, f32[8192,256]{0,1:T(8,128)}, f32[8192,256]{0,1:T(8,128)})) conditional(s32[]{:T(128)} %bitcast.118, (f32[1,256,2,8,128]{1,4,3,2,0:T(8,128)S(1)}, f32[8192,256]{0,1:T(8,128)}, f32[8192,256]{0,1:T(8,128)}) %tuple.106, (s32[]{:T(128)}, s32[12]{0:T(128)S(1)}, bf16[8704,256]{0,1:T(8,128)(2,1)}, ...), branch_computations={%region_10.10_spmd, %region_11.11_spmd} | conditional | flops 1352148224 | bytes 28486496 | solution.py:178
  224.2 2.4 fusion.18
  233.0 12.5 %conditional.7 = ((f32[1,256,2,8,128]{1,4,3,2,0:T(8,128)S(1)}, f32[8192,256]{0,1:T(8,128)}, f32[8192,256]{0,1:T(8,128)})) conditional(s32[]{:T(128)} %bitcast.118, (f32[1,256,2,8,128]{1,4,3,2,0:T(8,128)S(1)}, f32[8192,256]{0,1:T(8,128)}, f32[8192,256]{0,1:T(8,128)}) %tuple.106, (s32[]{:T(128)}, s32[12]{0:T(128)S(1)}, bf16[8704,256]{0,1:T(8,128)(2,1)}, ...), branch_computations={%region_10.10_spmd, %region_11.11_spmd} | conditional | flops 1352148224 | bytes 28486496 | solution.py:178
  238.1 2.4 fusion.18
  246.8 12.5 %conditional.7 = ((f32[1,256,2,8,128]{1,4,3,2,0:T(8,128)S(1)}, f32[8192,256]{0,1:T(8,128)}, f32[8192,256]{0,1:T(8,128)})) conditional(s32[]{:T(128)} %bitcast.118, (f32[1,256,2,8,128]{1,4,3,2,0:T(8,128)S(1)}, f32[8192,256]{0,1:T(8,128)}, f32[8192,256]{0,1:T(8,128)}) %tuple.106, (s32[]{:T(128)}, s32[12]{0:T(128)S(1)}, bf16[8704,256]{0,1:T(8,128)(2,1)}, ...), branch_computations={%region_10.10_spmd, %region_11.11_spmd} | conditional | flops 1352148224 | bytes 28486496 | solution.py:178
  251.9 2.4 fusion.18
  260.6 12.5 %conditional.7 = ((f32[1,256,2,8,128]{1,4,3,2,0:T(8,128)S(1)}, f32[8192,256]{0,1:T(8,128)}, f32[8192,256]{0,1:T(8,128)})) conditional(s32[]{:T(128)} %bitcast.118, (f32[1,256,2,8,128]{1,4,3,2,0:T(8,128)S(1)}, f32[8192,256]{0,1:T(8,128)}, f32[8192,256]{0,1:T(8,128)}) %tuple.106, (s32[]{:T(128)}, s32[12]{0:T(128)S(1)}, bf16[8704,256]{0,1:T(8,128)(2,1)}, ...), branch_computations={%region_10.10_spmd, %region_11.11_spmd} | conditional | flops 1352148224 | bytes 28486496 | solution.py:178
  265.7 2.4 fusion.18
  274.4 12.6 %conditional.7 = ((f32[1,256,2,8,128]{1,4,3,2,0:T(8,128)S(1)}, f32[8192,256]{0,1:T(8,128)}, f32[8192,256]{0,1:T(8,128)})) conditional(s32[]{:T(128)} %bitcast.118, (f32[1,256,2,8,128]{1,4,3,2,0:T(8,128)S(1)}, f32[8192,256]{0,1:T(8,128)}, f32[8192,256]{0,1:T(8,128)}) %tuple.106, (s32[]{:T(128)}, s32[12]{0:T(128)S(1)}, bf16[8704,256]{0,1:T(8,128)(2,1)}, ...), branch_computations={%region_10.10_spmd, %region_11.11_spmd} | conditional | flops 1352148224 | bytes 28486496 | solution.py:178
  279.5 2.4 fusion.18
  288.2 12.5 %conditional.7 = ((f32[1,256,2,8,128]{1,4,3,2,0:T(8,128)S(1)}, f32[8192,256]{0,1:T(8,128)}, f32[8192,256]{0,1:T(8,128)})) conditional(s32[]{:T(128)} %bitcast.118, (f32[1,256,2,8,128]{1,4,3,2,0:T(8,128)S(1)}, f32[8192,256]{0,1:T(8,128)}, f32[8192,256]{0,1:T(8,128)}) %tuple.106, (s32[]{:T(128)}, s32[12]{0:T(128)S(1)}, bf16[8704,256]{0,1:T(8,128)(2,1)}, ...), branch_computations={%region_10.10_spmd, %region_11.11_spmd} | conditional | flops 1352148224 | bytes 28486496 | solution.py:178
  293.3 2.4 fusion.18
  302.0 12.5 %conditional.7 = ((f32[1,256,2,8,128]{1,4,3,2,0:T(8,128)S(1)}, f32[8192,256]{0,1:T(8,128)}, f32[8192,256]{0,1:T(8,128)})) conditional(s32[]{:T(128)} %bitcast.118, (f32[1,256,2,8,128]{1,4,3,2,0:T(8,128)S(1)}, f32[8192,256]{0,1:T(8,128)}, f32[8192,256]{0,1:T(8,128)}) %tuple.106, (s32[]{:T(128)}, s32[12]{0:T(128)S(1)}, bf16[8704,256]{0,1:T(8,128)(2,1)}, ...), branch_computations={%region_10.10_spmd, %region_11.11_spmd} | conditional | flops 1352148224 | bytes 28486496 | solution.py:178
  307.1 2.4 fusion.18
  315.8 12.5 %conditional.7 = ((f32[1,256,2,8,128]{1,4,3,2,0:T(8,128)S(1)}, f32[8192,256]{0,1:T(8,128)}, f32[8192,256]{0,1:T(8,128)})) conditional(s32[]{:T(128)} %bitcast.118, (f32[1,256,2,8,128]{1,4,3,2,0:T(8,128)S(1)}, f32[8192,256]{0,1:T(8,128)}, f32[8192,256]{0,1:T(8,128)}) %tuple.106, (s32[]{:T(128)}, s32[12]{0:T(128)S(1)}, bf16[8704,256]{0,1:T(8,128)(2,1)}, ...), branch_computations={%region_10.10_spmd, %region_11.11_spmd} | conditional | flops 1352148224 | bytes 28486496 | solution.py:178
  320.9 2.4 fusion.18
  329.6 12.5 %conditional.7 = ((f32[1,256,2,8,128]{1,4,3,2,0:T(8,128)S(1)}, f32[8192,256]{0,1:T(8,128)}, f32[8192,256]{0,1:T(8,128)})) conditional(s32[]{:T(128)} %bitcast.118, (f32[1,256,2,8,128]{1,4,3,2,0:T(8,128)S(1)}, f32[8192,256]{0,1:T(8,128)}, f32[8192,256]{0,1:T(8,128)}) %tuple.106, (s32[]{:T(128)}, s32[12]{0:T(128)S(1)}, bf16[8704,256]{0,1:T(8,128)(2,1)}, ...), branch_computations={%region_10.10_spmd, %region_11.11_spmd} | conditional | flops 1352148224 | bytes 28486496 | solution.py:178
  334.7 2.4 fusion.18
  343.4 12.5 %conditional.7 = ((f32[1,256,2,8,128]{1,4,3,2,0:T(8,128)S(1)}, f32[8192,256]{0,1:T(8,128)}, f32[8192,256]{0,1:T(8,128)})) conditional(s32[]{:T(128)} %bitcast.118, (f32[1,256,2,8,128]{1,4,3,2,0:T(8,128)S(1)}, f32[8192,256]{0,1:T(8,128)}, f32[8192,256]{0,1:T(8,128)}) %tuple.106, (s32[]{:T(128)}, s32[12]{0:T(128)S(1)}, bf16[8704,256]{0,1:T(8,128)(2,1)}, ...), branch_computations={%region_10.10_spmd, %region_11.11_spmd} | conditional | flops 1352148224 | bytes 28486496 | solution.py:178
  348.5 2.4 fusion.18
  357.2 12.5 %conditional.7 = ((f32[1,256,2,8,128]{1,4,3,2,0:T(8,128)S(1)}, f32[8192,256]{0,1:T(8,128)}, f32[8192,256]{0,1:T(8,128)})) conditional(s32[]{:T(128)} %bitcast.118, (f32[1,256,2,8,128]{1,4,3,2,0:T(8,128)S(1)}, f32[8192,256]{0,1:T(8,128)}, f32[8192,256]{0,1:T(8,128)}) %tuple.106, (s32[]{:T(128)}, s32[12]{0:T(128)S(1)}, bf16[8704,256]{0,1:T(8,128)(2,1)}, ...), branch_computations={%region_10.10_spmd, %region_11.11_spmd} | conditional | flops 1352148224 | bytes 28486496 | solution.py:178
  371.0 12.5 %conditional.7 = ((f32[1,256,2,8,128]{1,4,3,2,0:T(8,128)S(1)}, f32[8192,256]{0,1:T(8,128)}, f32[8192,256]{0,1:T(8,128)})) conditional(s32[]{:T(128)} %bitcast.118, (f32[1,256,2,8,128]{1,4,3,2,0:T(8,128)S(1)}, f32[8192,256]{0,1:T(8,128)}, f32[8192,256]{0,1:T(8,128)}) %tuple.106, (s32[]{:T(128)}, s32[12]{0:T(128)S(1)}, bf16[8704,256]{0,1:T(8,128)(2,1)}, ...), branch_computations={%region_10.10_spmd, %region_11.11_spmd} | conditional | flops 1352148224 | bytes 28486496 | solution.py:178
  383.6 7.2 %copy.70 = bf16[8192,256]{1,0:T(8,128)(2,1)} copy(f32[8192,256]{0,1:T(8,128)} %get-tuple-element.595) | data formatting | bytes 12582912 | tf_op jit(solution)/shard_map/while | solution.py:182
  390.9 7.2 %copy.69 = bf16[8192,256]{1,0:T(8,128)(2,1)} copy(f32[8192,256]{0,1:T(8,128)} %get-tuple-element.594) | data formatting | bytes 12582912 | tf_op jit(solution)/shard_map/while | solution.py:182
  399.7 72.7 %reduce-scatter.5.cloned.1.call-done = bf16[256,256]{1,0:T(8,128)(2,1)} async-done(((bf16[8192,256]{1,0:T(8,128)(2,1)}), bf16[256,256]{1,0:T(8,128)(2,1)}) %reduce-scatter.5.cloned.1.call-update) | async-done | bytes 131088 | tf_op jit(solution)/shard_map/reduce_scatter | solution.py:187
  472.4 85.9 %reduce-scatter.3.cloned.1.call-done = bf16[256,256]{1,0:T(8,128)(2,1)} async-done(((bf16[8192,256]{1,0:T(8,128)(2,1)}), bf16[256,256]{1,0:T(8,128)(2,1)}) %reduce-scatter.3.cloned.1.call-update) | async-done | bytes 131088 | tf_op jit(solution)/shard_map/reduce_scatter | solution.py:184
  (515 shorter events, 209.3 us)
Async XLA Ops:
  7.2 7.5 %copy-start = (s32[32,12]{0,1:T(8,128)S(1)}, s32[32,12]{0,1:T(8,128)}, u32[]{:S(2)}) copy-start(s32[32,12]{0,1:T(8,128)} %param.29) | copy-start | bytes 4612
  7.2 12.0 %copy-start.3 = (bf16[256,2048]{1,0:T(8,128)(2,1)S(1)}, bf16[256,2048]{1,0:T(8,128)(2,1)}, u32[]{:S(2)}) copy-start(bf16[256,2048]{1,0:T(8,128)(2,1)} %param.26) | copy-start | bytes 3145732
  7.2 55.5 %all-gather.4.cloned.1.call-start = ((), (), s32[]{:S(2)}) async-start(), calls=%async_computation.2 | async-start | bytes 4325376 | tf_op jit(solution)/shard_map/all_gather | solution.py:125
  9.0 105.3 %all-gather.6.cloned.1.call-start = ((), (), s32[]{:S(2)}) async-start(), calls=%async_computation.3 | async-start | bytes 4325376 | tf_op jit(solution)/shard_map/all_gather | solution.py:126
  10.7 461.7 %reduce-scatter.5.cloned.1.call-start = ((), (), s32[]{:S(2)}) async-start(), calls=%async_computation.5 | async-start | bytes 4325376 | tf_op jit(solution)/shard_map/reduce_scatter | solution.py:187
  15.1 6.4 %copy-start.1 = (bf16[256,2048]{1,0:T(8,128)(2,1)S(1)}, bf16[256,2048]{1,0:T(8,128)(2,1)}, u32[]{:S(2)}) copy-start(bf16[256,2048]{1,0:T(8,128)(2,1)} %param.22) | copy-start | bytes 3145732
  17.6 5.2 copy-start.6
  17.6 6.3 %copy-start.5 = (s32[64]{0:T(128)S(1)}, s32[64]{0:T(128)}, u32[]{:S(2)}) copy-start(s32[64]{0:T(128)} %param.27) | copy-start | bytes 772
  17.6 41.2 %copy-start.4 = (s32[32]{0:T(128)S(1)}, s32[32]{0:T(128)}, u32[]{:S(2)}) copy-start(s32[32]{0:T(128)} %param.28) | copy-start | bytes 388
  226.6 1.6 copy-start.2
  240.4 1.6 copy-start.2
  254.3 1.6 copy-start.2
  268.1 1.6 copy-start.2
  281.9 1.6 copy-start.2
  295.7 1.6 copy-start.2
  309.5 1.6 copy-start.2
  323.3 1.6 copy-start.2
  337.1 1.6 copy-start.2
  350.9 1.6 copy-start.2
  364.7 1.6 copy-start.2
  378.5 1.6 copy-start.2
  390.8 167.5 %reduce-scatter.3.cloned.1.call-start = ((), (), s32[]{:S(2)}) async-start(), calls=%async_computation.4 | async-start | bytes 4325376 | tf_op jit(solution)/shard_map/reduce_scatter | solution.py:184
Sparse Core Ops, SparseCore 0:
  10.8 51.8 all-gather.3
  65.4 48.8 all-gather.5
  391.0 81.4 reduce-scatter.4
  477.0 81.2 reduce-scatter.2
where the time goes:
time: 568 us; the launch traced here: 565 us
  waiting for transfers between devices  214 us (38%)
  local copies, waits for them, and re-layouts  123 us (22%)
  matrix products  78.3 us (14%)
  other arithmetic  63.4 us (11%)
  loops' own time  34.9 us (6%)
  blocking collectives  34.6 us (6%)
  between operations  17 us (3%)
    reduce_scatter x1, waiting for transfers between devices, shards(): lax.psum_scatter(key_acc.astype(jnp.bfloat16), 'ctx', scatter_dimension=0...  85.9 us
    reduce_scatter x1, waiting for transfers between devices, shards(): lax.psum_scatter(value_acc.astype(jnp.bfloat16), 'ctx', scatter_dimension...  72.7 us
    all_gather x1, waiting for transfers between devices, shards(): lax.all_gather(values, 'ctx', axis=0, tiled=True)  51.6 us
    dot_general x24, matrix products, prepare(): jnp.einsum('ighd,jgd->ghij', query_four[local], key_tile, preferred_eleme...  40.6 us
    all_gather x1, blocking collectives, shards(): lax.all_gather(own_docs, 'ctx', axis=0, tiled=True)  25.6 us
    dynamic_slice x24, local copies, waits for them, and re-layouts, prepare(): lax.dynamic_slice_in_dim(padded_keys, begin, BLOCK, 0)  24.9 us
    dynamic_update_slice x12, other arithmetic, make_compute(): lax.dynamic_update_slice_in_dim(value_acc, old_values + value_grad.reshap...  22.7 us
    and x24, other arithmetic, prepare(): visible & (key_pos[None, :] <= query_pos[local][:, None])  18.2 us
  transfers between devices with their start and end apart: 4, of which 4 were waited for; matrix products, arithmetic and copies ran while one was open for 4% of the time, Pallas kernels for 0%

commit v1 on v0

v1 whole, which is shorter than its diff:
```python
import math

import jax
import jax.numpy as jnp
from jax import lax
from jax.experimental import pallas as pl
from jax.experimental.pallas import tpu as pltpu
from jax.sharding import PartitionSpec as P

HD = 128
BLOCK = 256
GROUP = 8
WIDE = GROUP * HD
SCALE = 1.0 / math.sqrt(HD)
FACTOR = SCALE * math.log2(math.e)
HIDE = -1e30
STAT_ROWS = 16


def index_of(z, y, core):
    return ((z % 4) * 4 + y % 4) * 2 + core


def pull(array, rz, ry):
    pairs = [
        (index_of(z + rz, y + ry, core), index_of(z, y, core))
        for z in range(4)
        for y in range(4)
        for core in range(2)
    ]
    return lax.ppermute(array, "ctx", pairs)


def push(array, rz, ry):
    return pull(array, -rz, -ry)


def swap(array):
    return lax.ppermute(array, "ctx", [(i, i ^ 1) for i in range(32)])


def halves(array, core, width):
    mine = lax.dynamic_slice_in_dim(array, core * width, width, 1)
    other = lax.dynamic_slice_in_dim(array, (1 - core) * width, width, 1)
    return mine, other


def dot(a, b, contract):
    return lax.dot_general(a, b, ((contract[:1], contract[1:]), ((), ())), preferred_element_type=jnp.float32)


def fill_bias(bias, starts, table, which, key_block):
    key_pos = key_block * BLOCK + lax.broadcasted_iota(jnp.int32, (BLOCK, BLOCK), 0)
    query_pos = table[3, which] * BLOCK + lax.broadcasted_iota(jnp.int32, (1, BLOCK), 1)
    seen = (key_pos >= starts[pl.ds(which, 1), :]) & (key_pos <= query_pos)
    bias[...] = jnp.where(seen, 0.0, HIDE)


def fill_starts(starts, firsts, table, bounds):
    for which in range(2):
        begin = table[3, which] * BLOCK
        pos = begin + lax.broadcasted_iota(jnp.int32, (1, BLOCK), 1)
        row = jnp.zeros((1, BLOCK), jnp.int32)
        first = jnp.int32(0)
        for k in range(4):
            edge = bounds[0, k]
            row = jnp.maximum(row, jnp.where(pos >= edge, edge, 0))
            first = jnp.maximum(first, jnp.where(begin >= edge, edge, 0))
        starts[pl.ds(which, 1), :] = row
        firsts[which] = first


def needed(table, firsts, which, j):
    return (table[1 + which, j] > 0) & (table[0, j] * BLOCK + BLOCK - 1 >= firsts[which])


def load_blocks(first_parts, second_parts, whole, sems, base):
    copies = []
    for n in range(4):
        copies.append(
            pltpu.make_async_copy(
                first_parts[n].at[:, pl.ds(0, BLOCK), :], whole.at[:, n, 0], sems.at[base + 2 * n]
            )
        )
        copies.append(
            pltpu.make_async_copy(
                second_parts[n].at[:, pl.ds(0, BLOCK), :], whole.at[n, :, 1], sems.at[base + 2 * n + 1]
            )
        )
    return copies


def stats_kernel(table, bounds, q0, q1, d0, d1, o0, o1, *rest):
    first_keys, second_keys = rest[0:4], rest[4:8]
    lse, delta = rest[8:10]
    keys_all, bias, starts, top, total, firsts, sems = rest[10:]
    copies = load_blocks(first_keys, second_keys, keys_all, sems, 0)
    for copy in copies:
        copy.start()
    fill_starts(starts, firsts, table, bounds)
    top[...] = jnp.full(top.shape, HIDE, jnp.float32)
    total[...] = jnp.zeros(total.shape, jnp.float32)
    for which, (d_ref, o_ref) in enumerate(((d0, o0), (d1, o1))):
        for h in range(GROUP):
            cols = pl.ds(h * HD, HD)
            product = d_ref[:, cols].astype(jnp.float32) * o_ref[:, cols].astype(jnp.float32)
            delta[pl.ds(which * GROUP + h, 1), :] = jnp.sum(product.T, axis=0, keepdims=True)
    for copy in copies:
        copy.wait()

    def one_key_block(j, carry):
        rz, ry, dc = j // 8, (j // 2) % 4, j % 2
        for which, q_ref in enumerate((q0, q1)):

            @pl.when(needed(table, firsts, which, j))
            def _():
                fill_bias(bias, starts, table, which, table[0, j])
                k = keys_all[rz, ry, dc]
                for h in range(GROUP):
                    row = which * GROUP + h
                    s = dot(k, q_ref[:, pl.ds(h * HD, HD)], (1, 1)) + bias[...]
                    s = s.reshape(BLOCK // 8, 8, BLOCK)
                    old = top[row]
                    new = jnp.maximum(old, jnp.max(s, axis=0))
                    weights = jnp.exp2((s - new[None]) * FACTOR)
                    total[row] = total[row] * jnp.exp2((old - new) * FACTOR) + jnp.sum(weights, axis=0)
                    top[row] = new

        return carry

    lax.fori_loop(0, 32, one_key_block, 0)
    for row in range(2 * GROUP):
        best = jnp.max(top[row], axis=0, keepdims=True)
        amount = jnp.sum(total[row] * jnp.exp2((top[row] - best) * FACTOR), axis=0, keepdims=True)
        lse[pl.ds(row, 1), :] = best * FACTOR + jnp.log2(amount)


def grads_kernel(table, bounds, lse, delta, q0, q1, d0, d1, *rest):
    first_keys, second_keys, first_values, second_values = (rest[4 * n : 4 * n + 4] for n in range(4))
    gq = rest[16:18]
    gk = rest[18:22]
    gv = rest[22:26]
    keys_all, values_all, gk_all, gv_all, gq_all, bias, key_turned, starts, firsts, sems = rest[26:]
    copies = load_blocks(first_keys, second_keys, keys_all, sems, 0)
    copies += load_blocks(first_values, second_values, values_all, sems, 8)
    for copy in copies:
        copy.start()
    fill_starts(starts, firsts, table, bounds)
    gq_all[...] = jnp.zeros(gq_all.shape, jnp.float32)
    for copy in copies:
        copy.wait()

    def one_key_block(j, carry):
        rz, ry, dc = j // 8, (j // 2) % 4, j % 2
        any_needed = needed(table, firsts, 0, j) | needed(table, firsts, 1, j)

        @pl.when(jnp.logical_not(any_needed))
        def _():
            gk_all[rz, ry, dc] = jnp.zeros((BLOCK, HD), jnp.bfloat16)
            gv_all[ry, rz, dc] = jnp.zeros((BLOCK, HD), jnp.bfloat16)

        @pl.when(any_needed)
        def _():
            key_turned[...] = keys_all[rz, ry, dc].astype(jnp.float32).T.astype(jnp.bfloat16)

        def add_query_block(which, q_ref, d_ref, gk_sum, gv_sum):
            fill_bias(bias, starts, table, which, table[0, j])
            k = keys_all[rz, ry, dc]
            v = values_all[rz, ry, dc]
            turned = key_turned[...]
            for h in range(GROUP):
                row = which * GROUP + h
                q = q_ref[:, pl.ds(h * HD, HD)]
                d = d_ref[:, pl.ds(h * HD, HD)]
                s = dot(k, q, (1, 1))
                p = jnp.exp2(s * FACTOR + bias[...] - lse[pl.ds(row, 1), :])
                dp = dot(v, d, (1, 1))
                ds = (p * (dp - delta[pl.ds(row, 1), :])).astype(jnp.bfloat16)
                gv_sum = gv_sum + dot(p.astype(jnp.bfloat16), d, (1, 0))
                gk_sum = gk_sum + dot(ds, q, (1, 0))
                gq_all[row] += dot(turned, ds, (1, 0))
            return gk_sum, gv_sum

        zero = jnp.zeros((BLOCK, HD), jnp.float32)
        sums = (zero, zero)
        for which, (q_ref, d_ref) in enumerate(((q0, d0), (q1, d1))):
            sums = lax.cond(
                needed(table, firsts, which, j),
                lambda a, b: add_query_block(which, q_ref, d_ref, a, b),
                lambda a, b: (a, b),
                *sums,
            )

        @pl.when(any_needed)
        def _():
            gk_all[rz, ry, dc] = (sums[0] * SCALE).astype(jnp.bfloat16)
            gv_all[ry, rz, dc] = sums[1].astype(jnp.bfloat16)

        return carry

    lax.fori_loop(0, 32, one_key_block, 0)
    outs = []
    for n in range(4):
        outs.append(pltpu.make_async_copy(gk_all.at[n], gk[n], sems.at[2 * n]))
        outs.append(pltpu.make_async_copy(gv_all.at[n], gv[n], sems.at[2 * n + 1]))
    for copy in outs:
        copy.start()
    for which in range(2):
        for h in range(GROUP):
            gq[which][:, pl.ds(h * HD, HD)] = (gq_all[which * GROUP + h] * SCALE).T.astype(jnp.bfloat16)
    for copy in outs:
        copy.wait()


SMEM = pl.BlockSpec(memory_space=pltpu.SMEM)
VMEM = pl.BlockSpec(memory_space=pltpu.VMEM)
ANY = pl.BlockSpec(memory_space=pl.ANY)
BIG = pltpu.CompilerParams(vmem_limit_bytes=50 * 1024 * 1024)


def row_stats(table, bounds, queries, grads, saved, first_keys, second_keys):
    return pl.pallas_call(
        stats_kernel,
        out_shape=[jax.ShapeDtypeStruct((2 * GROUP, BLOCK), jnp.float32)] * 2,
        in_specs=[SMEM] * 2 + [VMEM] * 6 + [ANY] * 8,
        out_specs=[VMEM] * 2,
        scratch_shapes=[
            pltpu.VMEM((4, 4, 2, BLOCK, HD), jnp.bfloat16),
            pltpu.VMEM((BLOCK, BLOCK), jnp.float32),
            pltpu.VMEM((8, BLOCK), jnp.int32),
            pltpu.VMEM((2 * GROUP, 8, BLOCK), jnp.float32),
            pltpu.VMEM((2 * GROUP, 8, BLOCK), jnp.float32),
            pltpu.SMEM((2,), jnp.int32),
            pltpu.SemaphoreType.DMA((8,)),
        ],
        compiler_params=BIG,
        cost_estimate=pl.CostEstimate(flops=2_000_000_000, bytes_accessed=5 << 20, transcendentals=8 << 20),
        name="row_stats",
    )(table, bounds, *queries, *grads, *saved, *first_keys, *second_keys)


def gradients(table, bounds, lse, delta, queries, grads, first_keys, second_keys, first_values, second_values):
    part = jax.ShapeDtypeStruct((4, 2, BLOCK, HD), jnp.bfloat16)
    return pl.pallas_call(
        grads_kernel,
        out_shape=[jax.ShapeDtypeStruct((BLOCK, WIDE), jnp.bfloat16)] * 2 + [part] * 8,
        in_specs=[SMEM] * 2 + [VMEM] * 6 + [ANY] * 16,
        out_specs=[VMEM] * 2 + [ANY] * 8,
        scratch_shapes=[
            pltpu.VMEM((4, 4, 2, BLOCK, HD), jnp.bfloat16),
            pltpu.VMEM((4, 4, 2, BLOCK, HD), jnp.bfloat16),
            pltpu.VMEM((4, 4, 2, BLOCK, HD), jnp.bfloat16),
            pltpu.VMEM((4, 4, 2, BLOCK, HD), jnp.bfloat16),
            pltpu.VMEM((2 * GROUP, HD, BLOCK), jnp.float32),
            pltpu.VMEM((BLOCK, BLOCK), jnp.float32),
            pltpu.VMEM((HD, BLOCK), jnp.bfloat16),
            pltpu.VMEM((8, BLOCK), jnp.int32),
            pltpu.SMEM((2,), jnp.int32),
            pltpu.SemaphoreType.DMA((16,)),
        ],
        compiler_params=BIG,
        cost_estimate=pl.CostEstimate(flops=10_000_000_000, bytes_accessed=10 << 20, transcendentals=8 << 20),
        name="gradients",
    )(table, bounds, lse, delta, *queries, *grads, *first_keys, *second_keys, *first_values, *second_values)


def gather_first(part):
    column = jnp.stack([part] + [pull(part, r, 0) for r in (1, 2, 3)])
    return [column] + [pull(column, 0, r) for r in (1, 2, 3)]


def gather_second(part):
    column = jnp.stack([part] + [pull(part, 0, r) for r in (1, 2, 3)])
    return [column] + [pull(column, r, 0) for r in (1, 2, 3)]


def add_up(arrays):
    total = arrays[0].astype(jnp.float32)
    for array in arrays[1:]:
        total = total + array.astype(jnp.float32)
    return total


def shards(query, keys, values, out_saved, d_out, doc_ids, placement, block_keys):
    me = lax.axis_index("ctx")
    core = me % 2
    x = lax.axis_index("head")
    z, y = me // 8, (me // 2) % 4

    pos = jnp.sum(jnp.where(jnp.arange(32) == me, placement, 0)) * BLOCK + x * 64 + jnp.arange(64)
    after = jnp.where(doc_ids[None, :] <= jnp.arange(128)[:, None] % 4, pos[None, :] + 1, 0)
    edges = jnp.max(after, axis=1)[None, :]
    for_x = [lax.ppermute(edges, "head", [(i, (i + r) % 4) for i in range(4)]) for r in (1, 2, 3)]
    edges = jnp.maximum(jnp.maximum(edges, for_x[0]), jnp.maximum(for_x[1], for_x[2]))
    stat_rows = jnp.concatenate([edges // 128, edges % 128, jnp.zeros((STAT_ROWS - 2, 128), jnp.int32)], axis=0)

    k_mine, k_other = halves(keys, core, HD)
    v_mine, v_other = halves(values, core, HD)
    q_mine, q_other = halves(query, core, WIDE)
    d_mine, d_other = halves(d_out, core, WIDE)
    o_mine, o_other = halves(out_saved, core, WIDE)
    k_swap = swap(k_other)
    v_swap = swap(v_other)
    queries = (q_mine, swap(q_other))
    grads = (d_mine, swap(d_other))
    saved = (o_mine, swap(o_other))

    first_keys = gather_first(jnp.concatenate([k_mine, stat_rows.astype(jnp.bfloat16)], axis=0))
    second_keys = gather_second(k_swap)
    first_values = gather_first(v_mine)
    second_values = gather_second(v_swap)

    seen = jnp.stack([part[:, BLOCK : BLOCK + 2, :] for part in first_keys]).astype(jnp.float32)
    bounds = jnp.max(seen[:, :, 0] * 128 + seen[:, :, 1], axis=(0, 1)).astype(jnp.int32)[None, :]
    bounds = jnp.maximum(bounds, swap(bounds))

    j = jnp.arange(32)
    slots = index_of(z + j // 8, y + (j // 2) % 4, core ^ (j % 2))
    block_of = jnp.sum(jnp.where(slots[:, None] == jnp.arange(32)[None, :], placement[None, :], 0), axis=1)
    own = block_of[:2]
    chosen = jnp.sum(
        jnp.where(own[:, None, None] == jnp.arange(32)[None, :, None], block_keys[None], 0), axis=1
    )
    listed = jnp.any(chosen[:, :, None] == block_of[None, None, :], axis=1).astype(jnp.int32)
    table = jnp.concatenate([block_of[None], listed, block_of[None]], axis=0).astype(jnp.int32)

    lse, delta = row_stats(table, bounds, queries, grads, saved, first_keys, second_keys)
    outs = gradients(
        table, bounds, lse, delta, queries, grads, first_keys, second_keys, first_values, second_values
    )
    gq_mine, gq_other, gk, gv = outs[0], outs[1], outs[2:6], outs[6:10]

    gq_swap = swap(gq_other)
    gk_line = add_up([gk[0]] + [push(gk[r], r, 0) for r in (1, 2, 3)]).astype(jnp.bfloat16)
    gv_line = add_up([gv[0]] + [push(gv[r], 0, r) for r in (1, 2, 3)]).astype(jnp.bfloat16)
    gk_here = add_up([gk_line[0]] + [push(gk_line[r], 0, r) for r in (1, 2, 3)]).astype(jnp.bfloat16)
    gv_here = add_up([gv_line[0]] + [push(gv_line[r], r, 0) for r in (1, 2, 3)]).astype(jnp.bfloat16)

    def join(mine, other):
        return jnp.where(
            core == 0, jnp.concatenate([mine, other], axis=1), jnp.concatenate([other, mine], axis=1)
        )

    return (
        join(gq_mine, gq_swap),
        join(gk_here[0], swap(gk_here[1])),
        join(gv_here[0], swap(gv_here[1])),
    )


def solution(mesh):
    placed = (
        P("ctx", "head"),
        P("ctx", "head"),
        P("ctx", "head"),
        P("ctx", "head"),
        P("ctx", "head"),
        P(("ctx", "head")),
        P(),
        P(),
    )
    return jax.shard_map(
        shards,
        mesh=mesh,
        in_specs=placed,
        out_specs=(P("ctx", "head"), P("ctx", "head"), P("ctx", "head")),
        check_vma=False,
    )
```

time: 568 us -> 190 us (0.33)
  waiting for transfers between devices: 214 us -> 61.2 us
  local copies, waits for them, and re-layouts: 123 us -> 6.06 us
  starting transfers between devices: 0.16 us -> 80.2 us
  matrix products: 78.3 us -> 0 us
  other arithmetic: 63.4 us -> 10.3 us
  loops' own time: 34.9 us -> 0 us
  blocking collectives: 34.6 us -> 0 us
  Pallas kernels: 0 us -> 29.8 us
  between operations: 17 us -> 1.76 us
    reduce_scatter x2 -> x0, waiting for transfers between devices: 159 us -> none  [the longest x1 85.9 us: shards(): lax.psum_scatter(key_acc.astype(jnp.bfloat16), 'ctx', scatter_dimension=0...]
    ppermute x0 -> x48, starting transfers between devices: none -> 80.2 us  [the longest x36 74.2 us: pull(): return lax.ppermute(array, 'ctx', pairs)]
    dynamic_slice x157 -> x5, local copies, waits for them, and re-layouts: 84.5 us -> 4.97 us  [halves(): other = lax.dynamic_slice_in_dim(array, (1 - core) * width, width, 1)]
    dot_general x72 -> x0, matrix products: 78.3 us -> none  [the longest x24 40.6 us: prepare(): jnp.einsum('ighd,jgd->ghij', query_four[local], key_tile, preferred_eleme...]
    ppermute x0 -> x48, waiting for transfers between devices: none -> 61.2 us  [the longest x36 59.2 us: pull(): return lax.ppermute(array, 'ctx', pairs)]
    all_gather x2 -> x0, waiting for transfers between devices: 55.4 us -> none  [the longest x1 51.6 us: shards(): lax.all_gather(values, 'ctx', axis=0, tiled=True)]
    another operation x26 -> x0, loops' own time: 34.9 us -> none  [the longest x12 9.25 us: add_tile_step(): lax.cond(intersections(tile_index, length), add_compute, lambda kept: kep...]
    pallas_call x0 -> x2, Pallas kernels: none -> 29.8 us  [the longest x1 21.7 us: gradients(): pl.pallas_call(grads_kernel, out_shape=[jax.ShapeDtypeStruct((BLOCK, WIDE...]
  transfers between devices with their start and end apart: 4 -> 48, of which waited for: 4 -> 18; matrix products, arithmetic and copies ran while one was open for 4% -> 7% of each run, Pallas kernels for 0% -> 4%
where the time goes in v1:
time: 190 us; the launch traced here: 189 us
  starting transfers between devices  80.2 us (42%)
  waiting for transfers between devices  61.2 us (32%)
  Pallas kernels  29.8 us (16%)
  other arithmetic  10.3 us (5%)
  local copies, waits for them, and re-layouts  6.06 us (3%)
    ppermute x36, starting transfers between devices, pull(): return lax.ppermute(array, 'ctx', pairs)  74.2 us
    ppermute x36, waiting for transfers between devices, pull(): return lax.ppermute(array, 'ctx', pairs)  59.2 us
    pallas_call x1, Pallas kernels, gradients(): pl.pallas_call(grads_kernel, out_shape=[jax.ShapeDtypeStruct((BLOCK, WIDE...  21.7 us
    pallas_call x1, Pallas kernels, row_stats(): pl.pallas_call(stats_kernel, out_shape=[jax.ShapeDtypeStruct((2 * GROUP,...  8.13 us
    ppermute x3, starting transfers between devices, shards(): lax.ppermute(edges, 'head', [(i, (i + r) % 4) for i in range(4)])  5.21 us
    dynamic_slice x5, local copies, waits for them, and re-layouts, halves(): other = lax.dynamic_slice_in_dim(array, (1 - core) * width, width, 1)  4.97 us
  transfers between devices with their start and end apart: 48, of which 18 were waited for; matrix products, arithmetic and copies ran while one was open for 7% of the time, Pallas kernels for 4%

profile of v1, /device:TPU:0, one launch (start us, length us, event | category | flops | bytes accessed | tf_op | source)
XLA Modules:
  0.0 189.4 jit_solution(14070413907423857954)
XLA Ops:
  0.7 1.3 fusion.9
  3.4 3.2 %collective-permute-start.1 = (s32[1,128]{1,0:T(1,128)S(1)}, s32[1,128]{1,0:T(1,128)S(1)}, u32[]{:S(2)}, u32[]{:S(2)}) collective-permute-start(s32[1,128]{1,0:T(1,128)S(1)} %bitcast.81), channel_id=1, source_target_pairs={{0,2},{1,3},{2,0},{3,1},{4,6},{5,7},{6,4},{7,5},{8,10},{9,11},{10,... | collective-permute-start | bytes 1544 | tf_op jit(solution)/shard_map/ppermute | solution.py:293
  6.6 1.1 collective-permute-start.2
  9.5 2.0 %collective-permute-start.22 = (bf16[256,128]{1,0:T(8,128)(2,1)S(1)}, bf16[256,128]{1,0:T(8,128)(2,1)S(1)}, u32[]{:S(2)}, u32[]{:S(2)}) collective-permute-start(bf16[256,128]{1,0:T(8,128)(2,1)S(1)} %get-tuple-element.46), channel_id=1, source_target_pairs={{96,0},{100,4},{104,8},{108,12},{112,16},{116,20},{120,24},{124,28... | collective-permute-start | bytes 196616 | tf_op jit(solution)/shard_map/ppermute | solution.py:31
  11.5 3.6 %collective-permute-start.21 = (bf16[256,128]{1,0:T(8,128)(2,1)S(1)}, bf16[256,128]{1,0:T(8,128)(2,1)S(1)}, u32[]{:S(2)}, u32[]{:S(2)}) collective-permute-start(bf16[256,128]{1,0:T(8,128)(2,1)S(1)} %get-tuple-element.46), channel_id=1, source_target_pairs={{64,0},{68,4},{72,8},{76,12},{80,16},{84,20},{88,24},{92,28},{96,3... | collective-permute-start | bytes 196616 | tf_op jit(solution)/shard_map/ppermute | solution.py:31
  16.0 2.2 %constant_dynamic-slice_fusion.7 = (bf16[256,1024]{1,0:T(8,128)(2,1)}, bf16[256,1024]{1,0:T(8,128)(2,1)S(1)}) fusion(bf16[256,2048]{1,0:T(8,128)(2,1)} %param.8, s32[]{:T(128)S(6)} %select_n.164, s32[]{:T(128)S(6)} %select_n.163), kind=kLoop, calls=%fused_computation.46 | loop fusion | bytes 2097160 | tf_op jit(solution)/shard_map/dynamic_slice | solution.py:44
  18.2 1.1 constant_dynamic-slice_fusion.3
  21.0 1.0 collective-permute-start.20
  23.8 3.1 %collective-permute-start.3 = (bf16[272,128]{1,0:T(8,128)(2,1)S(1)}, bf16[272,128]{1,0:T(8,128)(2,1)S(1)}, u32[]{:S(2)}, u32[]{:S(2)}) collective-permute-start(bf16[272,128]{1,0:T(8,128)(2,1)S(1)} %maximum_maximum_fusion), channel_id=1, source_target_pairs={{32,0},{36,4},{40,8},{44,12},{48,16},{52,20},{56,24},{60,28},{64,3... | collective-permute-start | bytes 208904 | tf_op jit(solution)/shard_map/ppermute | solution.py:31
  27.0 1.6 collective-permute-start.16
  29.2 3.2 %collective-permute-start.15 = (bf16[256,128]{1,0:T(8,128)(2,1)S(1)}, bf16[256,128]{1,0:T(8,128)(2,1)S(1)}, u32[]{:S(2)}, u32[]{:S(2)}) collective-permute-start(bf16[256,128]{1,0:T(8,128)(2,1)S(1)} %collective-permute-done.13), channel_id=1, source_target_pairs={{16,0},{20,4},{24,8},{28,12},{0,16},{4,20},{8,24},{12,28},{48,32},... | collective-permute-start | bytes 196616 | tf_op jit(solution)/shard_map/ppermute | solution.py:31
  32.4 1.1 collective-permute-start.14
  33.5 1.0 collective-permute-start.8
  34.6 1.3 collective-permute-start.25
  35.9 1.3 collective-permute-start.29
  37.1 2.3 %collective-permute-start.7 = (bf16[4,272,128]{2,1,0:T(8,128)(2,1)S(1)}, bf16[4,272,128]{2,1,0:T(8,128)(2,1)S(1)}, u32[]{:S(2)}, u32[]{:S(2)}) collective-permute-start(bf16[4,272,128]{2,1,0:T(8,128)(2,1)S(1)} %pad_maximum_fusion.rest_0_), channel_id=1, source_target_pairs={{16,0},{20,4},{24,8},{28,12},{0,16},{4,20},{8,24},{12,28},{48,32},... | collective-permute-start | bytes 835592 | tf_op jit(solution)/shard_map/ppermute | solution.py:31
  39.5 4.9 %collective-permute-done.8.rest_3_ = bf16[4,272,128]{2,1,0:T(8,128)(2,1)S(1)} collective-permute-done((bf16[4,272,128]{2,1,0:T(8,128)(2,1)S(1)}, bf16[4,272,128]{2,1,0:T(8,128)(2,1)S(1)}, u32[]{:S(2)}, u32[]{:S(2)}) %collective-permute-start.8) | collective-permute-done | bytes 278560 | tf_op jit(solution)/shard_map/ppermute | solution.py:31
  45.2 9.8 %collective-permute-done.7.rest_2_ = bf16[4,272,128]{2,1,0:T(8,128)(2,1)S(1)} collective-permute-done((bf16[4,272,128]{2,1,0:T(8,128)(2,1)S(1)}, bf16[4,272,128]{2,1,0:T(8,128)(2,1)S(1)}, u32[]{:S(2)}, u32[]{:S(2)}) %collective-permute-start.7) | collective-permute-done | bytes 278560 | tf_op jit(solution)/shard_map/ppermute | solution.py:31
  55.1 1.6 collective-permute-start.28
  56.8 4.0 %collective-permute-done.28 = bf16[256,128]{1,0:T(8,128)(2,1)S(1)} collective-permute-done((bf16[256,128]{1,0:T(8,128)(2,1)S(1)}, bf16[256,128]{1,0:T(8,128)(2,1)S(1)}, u32[]{:S(2)}, u32[]{:S(2)}) %collective-permute-start.28) | collective-permute-done | bytes 65568 | tf_op jit(solution)/shard_map/ppermute | solution.py:31
  60.9 1.1 collective-permute-start.19
  62.9 1.0 collective-permute-done.9
  64.0 2.9 %collective-permute-start.18 = (bf16[4,256,128]{2,1,0:T(8,128)(2,1)S(1)}, bf16[4,256,128]{2,1,0:T(8,128)(2,1)S(1)}, u32[]{:S(2)}, u32[]{:S(2)}) collective-permute-start(bf16[4,256,128]{2,1,0:T(8,128)(2,1)S(1)} %pad_maximum_fusion.1.rest_4_), channel_id=1, source_target_pairs={{64,0},{68,4},{72,8},{76,12},{80,16},{84,20},{88,24},{92,28},{96,3... | collective-permute-start | bytes 786440 | tf_op jit(solution)/shard_map/ppermute | solution.py:31
  66.9 5.5 %collective-permute-done.19.rest_7_ = bf16[4,256,128]{2,1,0:T(8,128)(2,1)} collective-permute-done((bf16[4,256,128]{2,1,0:T(8,128)(2,1)S(1)}, bf16[4,256,128]{2,1,0:T(8,128)(2,1)}, u32[]{:S(2)}, u32[]{:S(2)}) %collective-permute-start.19) | collective-permute-done | bytes 262176 | tf_op jit(solution)/shard_map/ppermute | solution.py:31
  72.9 0.9 pad_maximum_fusion.3.rest_12_
  73.9 2.5 %collective-permute-done.18.rest_6_ = bf16[4,256,128]{2,1,0:T(8,128)(2,1)S(1)} collective-permute-done((bf16[4,256,128]{2,1,0:T(8,128)(2,1)S(1)}, bf16[4,256,128]{2,1,0:T(8,128)(2,1)S(1)}, u32[]{:S(2)}, u32[]{:S(2)}) %collective-permute-start.18) | collective-permute-done | bytes 262176 | tf_op jit(solution)/shard_map/ppermute | solution.py:31
  76.4 2.4 %collective-permute-start.24 = (bf16[4,256,128]{2,1,0:T(8,128)(2,1)S(1)}, bf16[4,256,128]{2,1,0:T(8,128)(2,1)S(1)}, u32[]{:S(2)}, u32[]{:S(2)}) collective-permute-start(bf16[4,256,128]{2,1,0:T(8,128)(2,1)S(1)} %pad_maximum_fusion.2.rest_8_), channel_id=1, source_target_pairs={{16,0},{20,4},{24,8},{28,12},{0,16},{4,20},{8,24},{12,28},{48,32},... | collective-permute-start | bytes 786440 | tf_op jit(solution)/shard_map/ppermute | solution.py:31
  78.8 1.1 collective-permute-done.17.rest_5_
  80.2 0.9 collective-permute-start.32
  81.1 3.2 %collective-permute-start.31 = (bf16[4,256,128]{2,1,0:T(8,128)(2,1)S(1)}, bf16[4,256,128]{2,1,0:T(8,128)(2,1)S(1)}, u32[]{:S(2)}, u32[]{:S(2)}) collective-permute-start(bf16[4,256,128]{2,1,0:T(8,128)(2,1)S(1)} %pad_maximum_fusion.3.rest_12_), channel_id=1, source_target_pairs={{64,0},{68,4},{72,8},{76,12},{80,16},{84,20},{88,24},{92,28},{96,3... | collective-permute-start | bytes 786440 | tf_op jit(solution)/shard_map/ppermute | solution.py:31
  85.1 8.1 %row_stats.1 = (f32[16,256]{1,0:T(8,128)S(1)}, f32[16,256]{1,0:T(8,128)S(1)}) custom-call(s32[4,32]{1,0:T(4,128)S(1)} %pad_add_fusion.table, s32[1,128]{1,0:T(1,128)S(1)} %fusion.20.bounds, bf16[256,1024]{1,0:T(8,128)(2,1)S(1)} %get-tuple-element.34.q0, bf16[256,1024]{1,0:T(8,128)(2,1)S(1)} %collective-permute-done.10.q1, ...), custom_call_target="tpu_custom_call" | custom-call | flops 2000000000 | bytes 5242880 | tf_op jit(solution)/shard_map/row_stats/pallas_call | solution.py:222
  93.3 2.5 %collective-permute-done.31.rest_14_ = bf16[4,256,128]{2,1,0:T(8,128)(2,1)S(1)} collective-permute-done((bf16[4,256,128]{2,1,0:T(8,128)(2,1)S(1)}, bf16[4,256,128]{2,1,0:T(8,128)(2,1)S(1)}, u32[]{:S(2)}, u32[]{:S(2)}) %collective-permute-start.31) | collective-permute-done | bytes 262176 | tf_op jit(solution)/shard_map/ppermute | solution.py:31
  95.8 21.7 %gradients.1 = (bf16[256,1024]{1,0:T(8,128)(2,1)}, bf16[256,1024]{1,0:T(8,128)(2,1)}, bf16[4,2,256,128]{3,2,1,0:T(8,128)(2,1)}, bf16[4,2,256,128]{3,2,1,0:T(8,12...) custom-call(s32[4,32]{1,0:T(4,128)S(1)} %pad_add_fusion.table, ...), custom_call_target="tpu_custom_call" | custom-call | flops 10000000000 | bytes 10485760 | tf_op jit(solution)/shard_map/gradients/pallas_call | solution.py:244
  117.5 5.5 %collective-permute-start.34 = (bf16[4,2,256,128]{3,2,1,0:T(8,128)(2,1)}, bf16[4,2,256,128]{3,2,1,0:T(8,128)(2,1)S(1)}, u32[]{:S(2)}, u32[]{:S(2)}) collective-permute-start(bf16[4,2,256,128]{3,2,1,0:T(8,128)(2,1)} %get-tuple-element.20), channel_id=1, source_target_pairs={{96,0},{100,4},{104,8},{108,12},{112,16},{116,20},{120,24},{124,28... | collective-permute-start | bytes 1572872 | tf_op jit(solution)/shard_map/ppermute | solution.py:31
  122.9 2.8 %collective-permute-start.36 = (bf16[4,2,256,128]{3,2,1,0:T(8,128)(2,1)}, bf16[4,2,256,128]{3,2,1,0:T(8,128)(2,1)S(1)}, u32[]{:S(2)}, u32[]{:S(2)}) collective-permute-start(bf16[4,2,256,128]{3,2,1,0:T(8,128)(2,1)} %get-tuple-element.22), channel_id=1, source_target_pairs={{32,0},{36,4},{40,8},{44,12},{48,16},{52,20},{56,24},{60,28},{64,3... | collective-permute-start | bytes 1572872 | tf_op jit(solution)/shard_map/ppermute | solution.py:31
  125.7 1.5 collective-permute-start.41
  127.2 8.4 %collective-permute-done.34 = bf16[4,2,256,128]{3,2,1,0:T(8,128)(2,1)S(1)} collective-permute-done((bf16[4,2,256,128]{3,2,1,0:T(8,128)(2,1)}, bf16[4,2,256,128]{3,2,1,0:T(8,128)(2,1)S(1)}, u32[]{:S(2)}, u32[]{:S(2)}) %collective-permute-start.34) | collective-permute-done | bytes 524320 | tf_op jit(solution)/shard_map/ppermute | solution.py:31
  135.6 6.9 %collective-permute-start.42 = (bf16[4,2,256,128]{3,2,1,0:T(8,128)(2,1)}, bf16[4,2,256,128]{3,2,1,0:T(8,128)(2,1)S(1)}, u32[]{:S(2)}, u32[]{:S(2)}) collective-permute-start(bf16[4,2,256,128]{3,2,1,0:T(8,128)(2,1)} %get-tuple-element.25), channel_id=1, source_target_pairs={{16,0},{20,4},{24,8},{28,12},{0,16},{4,20},{8,24},{12,28},{48,32},... | collective-permute-start | bytes 1572872 | tf_op jit(solution)/shard_map/ppermute | solution.py:31
  142.5 2.8 %collective-permute-done.35 = bf16[4,2,256,128]{3,2,1,0:T(8,128)(2,1)S(1)} collective-permute-done((bf16[4,2,256,128]{3,2,1,0:T(8,128)(2,1)}, bf16[4,2,256,128]{3,2,1,0:T(8,128)(2,1)S(1)}, u32[]{:S(2)}, u32[]{:S(2)}) %collective-permute-start.35) | collective-permute-done | bytes 524320 | tf_op jit(solution)/shard_map/ppermute | solution.py:31
  145.3 13.7 %collective-permute-start.43 = (bf16[4,2,256,128]{3,2,1,0:T(8,128)(2,1)}, bf16[4,2,256,128]{3,2,1,0:T(8,128)(2,1)S(1)}, u32[]{:S(2)}, u32[]{:S(2)}) collective-permute-start(bf16[4,2,256,128]{3,2,1,0:T(8,128)(2,1)} %get-tuple-element.26), channel_id=1, source_target_pairs={{8,0},{12,4},{16,8},{20,12},{24,16},{28,20},{0,24},{4,28},{40,32},... | collective-permute-start | bytes 1572872 | tf_op jit(solution)/shard_map/ppermute | solution.py:31
  159.1 1.3 add_convert_fusion.1
  160.5 3.2 %collective-permute-start.39 = (bf16[2,256,128]{2,1,0:T(8,128)(2,1)S(1)}, bf16[2,256,128]{2,1,0:T(8,128)(2,1)S(1)}, u32[]{:S(2)}, u32[]{:S(2)}) collective-permute-start(bf16[2,256,128]{2,1,0:T(8,128)(2,1)S(1)} %get-tuple-element.39), channel_id=1, source_target_pairs={{8,0},{12,4},{16,8},{20,12},{24,16},{28,20},{0,24},{4,28},{40,32},... | collective-permute-start | bytes 393224 | tf_op jit(solution)/shard_map/ppermute | solution.py:31
  163.7 3.0 %collective-permute-done.42 = bf16[4,2,256,128]{3,2,1,0:T(8,128)(2,1)S(1)} collective-permute-done((bf16[4,2,256,128]{3,2,1,0:T(8,128)(2,1)}, bf16[4,2,256,128]{3,2,1,0:T(8,128)(2,1)S(1)}, u32[]{:S(2)}, u32[]{:S(2)}) %collective-permute-start.42) | collective-permute-done | bytes 524320 | tf_op jit(solution)/shard_map/ppermute | solution.py:31
  166.7 9.1 %collective-permute-done.43 = bf16[4,2,256,128]{3,2,1,0:T(8,128)(2,1)S(1)} collective-permute-done((bf16[4,2,256,128]{3,2,1,0:T(8,128)(2,1)}, bf16[4,2,256,128]{3,2,1,0:T(8,128)(2,1)S(1)}, u32[]{:S(2)}, u32[]{:S(2)}) %collective-permute-start.43) | collective-permute-done | bytes 524320 | tf_op jit(solution)/shard_map/ppermute | solution.py:31
  176.3 3.2 %collective-permute-start.46 = (bf16[2,256,128]{2,1,0:T(8,128)(2,1)S(1)}, bf16[2,256,128]{2,1,0:T(8,128)(2,1)S(1)}, u32[]{:S(2)}, u32[]{:S(2)}) collective-permute-start(bf16[2,256,128]{2,1,0:T(8,128)(2,1)S(1)} %get-tuple-element.36), channel_id=1, source_target_pairs={{32,0},{36,4},{40,8},{44,12},{48,16},{52,20},{56,24},{60,28},{64,3... | collective-permute-start | bytes 393224 | tf_op jit(solution)/shard_map/ppermute | solution.py:31
  179.5 1.4 maximum_select_fusion
  180.8 1.3 collective-permute-start.45
  183.0 4.3 %collective-permute-done.45 = bf16[2,256,128]{2,1,0:T(8,128)(2,1)S(1)} collective-permute-done((bf16[2,256,128]{2,1,0:T(8,128)(2,1)S(1)}, bf16[2,256,128]{2,1,0:T(8,128)(2,1)S(1)}, u32[]{:S(2)}, u32[]{:S(2)}) %collective-permute-start.45) | collective-permute-done | bytes 131104 | tf_op jit(solution)/shard_map/ppermute | solution.py:31
  (123 shorter events, 14.8 us)
Async XLA Ops:
  3.4 17.6 %collective-permute-start.1 = (s32[1,128]{1,0:T(1,128)S(1)}, s32[1,128]{1,0:T(1,128)S(1)}, u32[]{:S(2)}, u32[]{:S(2)}) collective-permute-start(s32[1,128]{1,0:T(1,128)S(1)} %bitcast.81), channel_id=1, source_target_pairs={{0,2},{1,3},{2,0},{3,1},{4,6},{5,7},{6,4},{7,5},{8,10},{9,11},{10,... | collective-permute-start | bytes 1544 | tf_op jit(solution)/shard_map/ppermute | solution.py:293
  6.6 15.4 %collective-permute-start.2 = (s32[1,128]{1,0:T(1,128)S(1)}, s32[1,128]{1,0:T(1,128)S(1)}, u32[]{:S(2)}, u32[]{:S(2)}) collective-permute-start(s32[1,128]{1,0:T(1,128)S(1)} %bitcast.82), channel_id=1, source_target_pairs={{0,3},{1,0},{2,1},{3,2},{4,7},{5,4},{6,5},{7,6},{8,11},{9,8},{10,9... | collective-permute-start | bytes 1544 | tf_op jit(solution)/shard_map/ppermute | solution.py:293
  7.8 14.3 %collective-permute-start = (s32[1,128]{1,0:T(1,128)S(1)}, s32[1,128]{1,0:T(1,128)S(1)}, u32[]{:S(2)}, u32[]{:S(2)}) collective-permute-start(s32[1,128]{1,0:T(1,128)S(1)} %bitcast.83), channel_id=1, source_target_pairs={{0,1},{1,2},{2,3},{3,0},{4,5},{5,6},{6,7},{7,4},{8,9},{9,10},{10,1... | collective-permute-start | bytes 1544 | tf_op jit(solution)/shard_map/ppermute | solution.py:293
  9.5 14.3 %collective-permute-start.22 = (bf16[256,128]{1,0:T(8,128)(2,1)S(1)}, bf16[256,128]{1,0:T(8,128)(2,1)S(1)}, u32[]{:S(2)}, u32[]{:S(2)}) collective-permute-start(bf16[256,128]{1,0:T(8,128)(2,1)S(1)} %get-tuple-element.46), channel_id=1, source_target_pairs={{96,0},{100,4},{104,8},{108,12},{112,16},{116,20},{120,24},{124,28... | collective-permute-start | bytes 196616 | tf_op jit(solution)/shard_map/ppermute | solution.py:31
  11.5 15.5 %collective-permute-start.21 = (bf16[256,128]{1,0:T(8,128)(2,1)S(1)}, bf16[256,128]{1,0:T(8,128)(2,1)S(1)}, u32[]{:S(2)}, u32[]{:S(2)}) collective-permute-start(bf16[256,128]{1,0:T(8,128)(2,1)S(1)} %get-tuple-element.46), channel_id=1, source_target_pairs={{64,0},{68,4},{72,8},{76,12},{80,16},{84,20},{88,24},{92,28},{96,3... | collective-permute-start | bytes 196616 | tf_op jit(solution)/shard_map/ppermute | solution.py:31
  21.0 6.0 %collective-permute-start.20 = (bf16[256,128]{1,0:T(8,128)(2,1)S(1)}, bf16[256,128]{1,0:T(8,128)(2,1)S(1)}, u32[]{:S(2)}, u32[]{:S(2)}) collective-permute-start(bf16[256,128]{1,0:T(8,128)(2,1)S(1)} %get-tuple-element.46), channel_id=1, source_target_pairs={{32,0},{36,4},{40,8},{44,12},{48,16},{52,20},{56,24},{60,28},{64,3... | collective-permute-start | bytes 196616 | tf_op jit(solution)/shard_map/ppermute | solution.py:31
  22.0 1.3 collective-permute-start.13
  22.0 12.5 %collective-permute-start.26 = (bf16[256,128]{1,0:T(8,128)(2,1)S(1)}, bf16[256,128]{1,0:T(8,128)(2,1)S(1)}, u32[]{:S(2)}, u32[]{:S(2)}) collective-permute-start(bf16[256,128]{1,0:T(8,128)(2,1)S(1)} %get-tuple-element.45), channel_id=1, source_target_pairs={{0,4},{4,0},{8,12},{12,8},{16,20},{20,16},{24,28},{28,24},{32,36},... | collective-permute-start | bytes 196616 | tf_op jit(solution)/shard_map/ppermute | solution.py:39
  23.3 5.9 %collective-permute-start.4 = (bf16[272,128]{1,0:T(8,128)(2,1)S(1)}, bf16[272,128]{1,0:T(8,128)(2,1)S(1)}, u32[]{:S(2)}, u32[]{:S(2)}) collective-permute-start(bf16[272,128]{1,0:T(8,128)(2,1)S(1)} %maximum_maximum_fusion), channel_id=1, source_target_pairs={{64,0},{68,4},{72,8},{76,12},{80,16},{84,20},{88,24},{92,28},{96,3... | collective-permute-start | bytes 208904 | tf_op jit(solution)/shard_map/ppermute | solution.py:31
  23.8 8.6 %collective-permute-start.3 = (bf16[272,128]{1,0:T(8,128)(2,1)S(1)}, bf16[272,128]{1,0:T(8,128)(2,1)S(1)}, u32[]{:S(2)}, u32[]{:S(2)}) collective-permute-start(bf16[272,128]{1,0:T(8,128)(2,1)S(1)} %maximum_maximum_fusion), channel_id=1, source_target_pairs={{32,0},{36,4},{40,8},{44,12},{48,16},{52,20},{56,24},{60,28},{64,3... | collective-permute-start | bytes 208904 | tf_op jit(solution)/shard_map/ppermute | solution.py:31
  27.0 6.5 %collective-permute-start.5 = (bf16[272,128]{1,0:T(8,128)(2,1)S(1)}, bf16[272,128]{1,0:T(8,128)(2,1)S(1)}, u32[]{:S(2)}, u32[]{:S(2)}) collective-permute-start(bf16[272,128]{1,0:T(8,128)(2,1)S(1)} %maximum_maximum_fusion), channel_id=1, source_target_pairs={{96,0},{100,4},{104,8},{108,12},{112,16},{116,20},{120,24},{124,28... | collective-permute-start | bytes 208904 | tf_op jit(solution)/shard_map/ppermute | solution.py:31
  27.0 7.6 %collective-permute-start.16 = (bf16[256,128]{1,0:T(8,128)(2,1)S(1)}, bf16[256,128]{1,0:T(8,128)(2,1)S(1)}, u32[]{:S(2)}, u32[]{:S(2)}) collective-permute-start(bf16[256,128]{1,0:T(8,128)(2,1)S(1)} %collective-permute-done.13), channel_id=1, source_target_pairs={{24,0},{28,4},{0,8},{4,12},{8,16},{12,20},{16,24},{20,28},{56,32},... | collective-permute-start | bytes 196616 | tf_op jit(solution)/shard_map/ppermute | solution.py:31
  29.2 6.6 %collective-permute-start.15 = (bf16[256,128]{1,0:T(8,128)(2,1)S(1)}, bf16[256,128]{1,0:T(8,128)(2,1)S(1)}, u32[]{:S(2)}, u32[]{:S(2)}) collective-permute-start(bf16[256,128]{1,0:T(8,128)(2,1)S(1)} %collective-permute-done.13), channel_id=1, source_target_pairs={{16,0},{20,4},{24,8},{28,12},{0,16},{4,20},{8,24},{12,28},{48,32},... | collective-permute-start | bytes 196616 | tf_op jit(solution)/shard_map/ppermute | solution.py:31
  32.4 4.7 %collective-permute-start.14 = (bf16[256,128]{1,0:T(8,128)(2,1)S(1)}, bf16[256,128]{1,0:T(8,128)(2,1)S(1)}, u32[]{:S(2)}, u32[]{:S(2)}) collective-permute-start(bf16[256,128]{1,0:T(8,128)(2,1)S(1)} %collective-permute-done.13), channel_id=1, source_target_pairs={{8,0},{12,4},{16,8},{20,12},{24,16},{28,20},{0,24},{4,28},{40,32},... | collective-permute-start | bytes 196616 | tf_op jit(solution)/shard_map/ppermute | solution.py:31
  33.5 10.9 %collective-permute-start.8 = (bf16[4,272,128]{2,1,0:T(8,128)(2,1)S(1)}, bf16[4,272,128]{2,1,0:T(8,128)(2,1)S(1)}, u32[]{:S(2)}, u32[]{:S(2)}) collective-permute-start(bf16[4,272,128]{2,1,0:T(8,128)(2,1)S(1)} %pad_maximum_fusion.rest_0_), channel_id=1, source_target_pairs={{24,0},{28,4},{0,8},{4,12},{8,16},{12,20},{16,24},{20,28},{56,32},... | collective-permute-start | bytes 835592 | tf_op jit(solution)/shard_map/ppermute | solution.py:31
  34.6 45.7 %collective-permute-start.10 = (bf16[256,1024]{1,0:T(8,128)(2,1)}, bf16[256,1024]{1,0:T(8,128)(2,1)S(1)}, u32[]{:S(2)}, u32[]{:S(2)}) collective-permute-start(bf16[256,1024]{1,0:T(8,128)(2,1)} %get-tuple-element.33), channel_id=1, source_target_pairs={{0,4},{4,0},{8,12},{12,8},{16,20},{20,16},{24,28},{28,24},{32,36},... | collective-permute-start | bytes 1572872 | tf_op jit(solution)/shard_map/ppermute | solution.py:39
  34.6 27.9 %collective-permute-start.25 = (bf16[4,256,128]{2,1,0:T(8,128)(2,1)S(1)}, bf16[4,256,128]{2,1,0:T(8,128)(2,1)S(1)}, u32[]{:S(2)}, u32[]{:S(2)}) collective-permute-start(bf16[4,256,128]{2,1,0:T(8,128)(2,1)S(1)} %pad_maximum_fusion.2.rest_8_), channel_id=1, source_target_pairs={{24,0},{28,4},{0,8},{4,12},{8,16},{12,20},{16,24},{20,28},{56,32},... | collective-permute-start | bytes 786440 | tf_op jit(solution)/shard_map/ppermute | solution.py:31
  35.9 20.9 %collective-permute-start.29 = (bf16[256,128]{1,0:T(8,128)(2,1)S(1)}, bf16[256,128]{1,0:T(8,128)(2,1)S(1)}, u32[]{:S(2)}, u32[]{:S(2)}) collective-permute-start(bf16[256,128]{1,0:T(8,128)(2,1)S(1)} %collective-permute-done.26), channel_id=1, source_target_pairs={{24,0},{28,4},{0,8},{4,12},{8,16},{12,20},{16,24},{20,28},{56,32},... | collective-permute-start | bytes 196616 | tf_op jit(solution)/shard_map/ppermute | solution.py:31
  37.1 17.9 %collective-permute-start.7 = (bf16[4,272,128]{2,1,0:T(8,128)(2,1)S(1)}, bf16[4,272,128]{2,1,0:T(8,128)(2,1)S(1)}, u32[]{:S(2)}, u32[]{:S(2)}) collective-permute-start(bf16[4,272,128]{2,1,0:T(8,128)(2,1)S(1)} %pad_maximum_fusion.rest_0_), channel_id=1, source_target_pairs={{16,0},{20,4},{24,8},{28,12},{0,16},{4,20},{8,24},{12,28},{48,32},... | collective-permute-start | bytes 835592 | tf_op jit(solution)/shard_map/ppermute | solution.py:31
  44.4 12.2 %collective-permute-start.6 = (bf16[4,272,128]{2,1,0:T(8,128)(2,1)S(1)}, bf16[4,272,128]{2,1,0:T(8,128)(2,1)S(1)}, u32[]{:S(2)}, u32[]{:S(2)}) collective-permute-start(bf16[4,272,128]{2,1,0:T(8,128)(2,1)S(1)} %pad_maximum_fusion.rest_0_), channel_id=1, source_target_pairs={{8,0},{12,4},{16,8},{20,12},{24,16},{28,20},{0,24},{4,28},{40,32},... | collective-permute-start | bytes 835592 | tf_op jit(solution)/shard_map/ppermute | solution.py:31
  55.1 5.8 %collective-permute-start.28 = (bf16[256,128]{1,0:T(8,128)(2,1)S(1)}, bf16[256,128]{1,0:T(8,128)(2,1)S(1)}, u32[]{:S(2)}, u32[]{:S(2)}) collective-permute-start(bf16[256,128]{1,0:T(8,128)(2,1)S(1)} %collective-permute-done.26), channel_id=1, source_target_pairs={{16,0},{20,4},{24,8},{28,12},{0,16},{4,20},{8,24},{12,28},{48,32},... | collective-permute-start | bytes 196616 | tf_op jit(solution)/shard_map/ppermute | solution.py:31
  56.6 4.3 %collective-permute-start.27 = (bf16[256,128]{1,0:T(8,128)(2,1)S(1)}, bf16[256,128]{1,0:T(8,128)(2,1)S(1)}, u32[]{:S(2)}, u32[]{:S(2)}) collective-permute-start(bf16[256,128]{1,0:T(8,128)(2,1)S(1)} %collective-permute-done.26), channel_id=1, source_target_pairs={{8,0},{12,4},{16,8},{20,12},{24,16},{28,20},{0,24},{4,28},{40,32},... | collective-permute-start | bytes 196616 | tf_op jit(solution)/shard_map/ppermute | solution.py:31
  56.7 24.4 %collective-permute-start.12 = (bf16[256,1024]{1,0:T(8,128)(2,1)}, bf16[256,1024]{1,0:T(8,128)(2,1)}, u32[]{:S(2)}, u32[]{:S(2)}) collective-permute-start(bf16[256,1024]{1,0:T(8,128)(2,1)} %get-tuple-element.29), channel_id=1, source_target_pairs={{0,4},{4,0},{8,12},{12,8},{16,20},{20,16},{24,28},{28,24},{32,36},... | collective-permute-start | bytes 1572872 | tf_op jit(solution)/shard_map/ppermute | solution.py:39
  60.8 23.5 %collective-permute-start.11 = (bf16[256,1024]{1,0:T(8,128)(2,1)}, bf16[256,1024]{1,0:T(8,128)(2,1)}, u32[]{:S(2)}, u32[]{:S(2)}) collective-permute-start(bf16[256,1024]{1,0:T(8,128)(2,1)} %get-tuple-element.31), channel_id=1, source_target_pairs={{0,4},{4,0},{8,12},{12,8},{16,20},{20,16},{24,28},{28,24},{32,36},... | collective-permute-start | bytes 1572872 | tf_op jit(solution)/shard_map/ppermute | solution.py:39
  60.9 11.4 %collective-permute-start.19 = (bf16[4,256,128]{2,1,0:T(8,128)(2,1)S(1)}, bf16[4,256,128]{2,1,0:T(8,128)(2,1)}, u32[]{:S(2)}, u32[]{:S(2)}) collective-permute-start(bf16[4,256,128]{2,1,0:T(8,128)(2,1)S(1)} %pad_maximum_fusion.1.rest_4_), channel_id=1, source_target_pairs={{96,0},{100,4},{104,8},{108,12},{112,16},{116,20},{120,24},{124,28... | collective-permute-start | bytes 786440 | tf_op jit(solution)/shard_map/ppermute | solution.py:31
  62.5 1.5 collective-permute-start.9
  64.0 12.4 %collective-permute-start.18 = (bf16[4,256,128]{2,1,0:T(8,128)(2,1)S(1)}, bf16[4,256,128]{2,1,0:T(8,128)(2,1)S(1)}, u32[]{:S(2)}, u32[]{:S(2)}) collective-permute-start(bf16[4,256,128]{2,1,0:T(8,128)(2,1)S(1)} %pad_maximum_fusion.1.rest_4_), channel_id=1, source_target_pairs={{64,0},{68,4},{72,8},{76,12},{80,16},{84,20},{88,24},{92,28},{96,3... | collective-permute-start | bytes 786440 | tf_op jit(solution)/shard_map/ppermute | solution.py:31
  72.4 7.5 %collective-permute-start.17 = (bf16[4,256,128]{2,1,0:T(8,128)(2,1)S(1)}, bf16[4,256,128]{2,1,0:T(8,128)(2,1)S(1)}, u32[]{:S(2)}, u32[]{:S(2)}) collective-permute-start(bf16[4,256,128]{2,1,0:T(8,128)(2,1)S(1)} %pad_maximum_fusion.1.rest_4_), channel_id=1, source_target_pairs={{32,0},{36,4},{40,8},{44,12},{48,16},{52,20},{56,24},{60,28},{64,3... | collective-permute-start | bytes 786440 | tf_op jit(solution)/shard_map/ppermute | solution.py:31
  76.4 16.9 %collective-permute-start.24 = (bf16[4,256,128]{2,1,0:T(8,128)(2,1)S(1)}, bf16[4,256,128]{2,1,0:T(8,128)(2,1)S(1)}, u32[]{:S(2)}, u32[]{:S(2)}) collective-permute-start(bf16[4,256,128]{2,1,0:T(8,128)(2,1)S(1)} %pad_maximum_fusion.2.rest_8_), channel_id=1, source_target_pairs={{16,0},{20,4},{24,8},{28,12},{0,16},{4,20},{8,24},{12,28},{48,32},... | collective-permute-start | bytes 786440 | tf_op jit(solution)/shard_map/ppermute | solution.py:31
  79.8 13.4 %collective-permute-start.23 = (bf16[4,256,128]{2,1,0:T(8,128)(2,1)S(1)}, bf16[4,256,128]{2,1,0:T(8,128)(2,1)S(1)}, u32[]{:S(2)}, u32[]{:S(2)}) collective-permute-start(bf16[4,256,128]{2,1,0:T(8,128)(2,1)S(1)} %pad_maximum_fusion.2.rest_8_), channel_id=1, source_target_pairs={{8,0},{12,4},{16,8},{20,12},{24,16},{28,20},{0,24},{4,28},{40,32},... | collective-permute-start | bytes 786440 | tf_op jit(solution)/shard_map/ppermute | solution.py:31
  80.2 13.1 %collective-permute-start.32 = (bf16[4,256,128]{2,1,0:T(8,128)(2,1)S(1)}, bf16[4,256,128]{2,1,0:T(8,128)(2,1)S(1)}, u32[]{:S(2)}, u32[]{:S(2)}) collective-permute-start(bf16[4,256,128]{2,1,0:T(8,128)(2,1)S(1)} %pad_maximum_fusion.3.rest_12_), channel_id=1, source_target_pairs={{96,0},{100,4},{104,8},{108,12},{112,16},{116,20},{120,24},{124,28... | collective-permute-start | bytes 786440 | tf_op jit(solution)/shard_map/ppermute | solution.py:31
  81.1 14.6 %collective-permute-start.31 = (bf16[4,256,128]{2,1,0:T(8,128)(2,1)S(1)}, bf16[4,256,128]{2,1,0:T(8,128)(2,1)S(1)}, u32[]{:S(2)}, u32[]{:S(2)}) collective-permute-start(bf16[4,256,128]{2,1,0:T(8,128)(2,1)S(1)} %pad_maximum_fusion.3.rest_12_), channel_id=1, source_target_pairs={{64,0},{68,4},{72,8},{76,12},{80,16},{84,20},{88,24},{92,28},{96,3... | collective-permute-start | bytes 786440 | tf_op jit(solution)/shard_map/ppermute | solution.py:31
  84.3 11.4 %collective-permute-start.30 = (bf16[4,256,128]{2,1,0:T(8,128)(2,1)S(1)}, bf16[4,256,128]{2,1,0:T(8,128)(2,1)S(1)}, u32[]{:S(2)}, u32[]{:S(2)}) collective-permute-start(bf16[4,256,128]{2,1,0:T(8,128)(2,1)S(1)} %pad_maximum_fusion.3.rest_12_), channel_id=1, source_target_pairs={{32,0},{36,4},{40,8},{44,12},{48,16},{52,20},{56,24},{60,28},{64,3... | collective-permute-start | bytes 786440 | tf_op jit(solution)/shard_map/ppermute | solution.py:31
  117.5 18.2 %collective-permute-start.34 = (bf16[4,2,256,128]{3,2,1,0:T(8,128)(2,1)}, bf16[4,2,256,128]{3,2,1,0:T(8,128)(2,1)S(1)}, u32[]{:S(2)}, u32[]{:S(2)}) collective-permute-start(bf16[4,2,256,128]{3,2,1,0:T(8,128)(2,1)} %get-tuple-element.20), channel_id=1, source_target_pairs={{96,0},{100,4},{104,8},{108,12},{112,16},{116,20},{120,24},{124,28... | collective-permute-start | bytes 1572872 | tf_op jit(solution)/shard_map/ppermute | solution.py:31
  122.9 22.4 %collective-permute-start.35 = (bf16[4,2,256,128]{3,2,1,0:T(8,128)(2,1)}, bf16[4,2,256,128]{3,2,1,0:T(8,128)(2,1)S(1)}, u32[]{:S(2)}, u32[]{:S(2)}) collective-permute-start(bf16[4,2,256,128]{3,2,1,0:T(8,128)(2,1)} %get-tuple-element.21), channel_id=1, source_target_pairs={{64,0},{68,4},{72,8},{76,12},{80,16},{84,20},{88,24},{92,28},{96,3... | collective-permute-start | bytes 1572872 | tf_op jit(solution)/shard_map/ppermute | solution.py:31
  122.9 36.1 %collective-permute-start.36 = (bf16[4,2,256,128]{3,2,1,0:T(8,128)(2,1)}, bf16[4,2,256,128]{3,2,1,0:T(8,128)(2,1)S(1)}, u32[]{:S(2)}, u32[]{:S(2)}) collective-permute-start(bf16[4,2,256,128]{3,2,1,0:T(8,128)(2,1)} %get-tuple-element.22), channel_id=1, source_target_pairs={{32,0},{36,4},{40,8},{44,12},{48,16},{52,20},{56,24},{60,28},{64,3... | collective-permute-start | bytes 1572872 | tf_op jit(solution)/shard_map/ppermute | solution.py:31
  125.7 50.6 %collective-permute-start.33 = (bf16[256,1024]{1,0:T(8,128)(2,1)}, bf16[256,1024]{1,0:T(8,128)(2,1)S(1)}, u32[]{:S(2)}, u32[]{:S(2)}) collective-permute-start(bf16[256,1024]{1,0:T(8,128)(2,1)} %get-tuple-element.18), channel_id=1, source_target_pairs={{0,4},{4,0},{8,12},{12,8},{16,20},{20,16},{24,28},{28,24},{32,36},... | collective-permute-start | bytes 1572872 | tf_op jit(solution)/shard_map/ppermute | solution.py:39
  125.7 34.8 %collective-permute-start.41 = (bf16[4,2,256,128]{3,2,1,0:T(8,128)(2,1)}, bf16[4,2,256,128]{3,2,1,0:T(8,128)(2,1)S(1)}, u32[]{:S(2)}, u32[]{:S(2)}) collective-permute-start(bf16[4,2,256,128]{3,2,1,0:T(8,128)(2,1)} %get-tuple-element.24), channel_id=1, source_target_pairs={{24,0},{28,4},{0,8},{4,12},{8,16},{12,20},{16,24},{20,28},{56,32},... | collective-permute-start | bytes 1572872 | tf_op jit(solution)/shard_map/ppermute | solution.py:31
  135.6 31.1 %collective-permute-start.42 = (bf16[4,2,256,128]{3,2,1,0:T(8,128)(2,1)}, bf16[4,2,256,128]{3,2,1,0:T(8,128)(2,1)S(1)}, u32[]{:S(2)}, u32[]{:S(2)}) collective-permute-start(bf16[4,2,256,128]{3,2,1,0:T(8,128)(2,1)} %get-tuple-element.25), channel_id=1, source_target_pairs={{16,0},{20,4},{24,8},{28,12},{0,16},{4,20},{8,24},{12,28},{48,32},... | collective-permute-start | bytes 1572872 | tf_op jit(solution)/shard_map/ppermute | solution.py:31
  145.3 30.5 %collective-permute-start.43 = (bf16[4,2,256,128]{3,2,1,0:T(8,128)(2,1)}, bf16[4,2,256,128]{3,2,1,0:T(8,128)(2,1)S(1)}, u32[]{:S(2)}, u32[]{:S(2)}) collective-permute-start(bf16[4,2,256,128]{3,2,1,0:T(8,128)(2,1)} %get-tuple-element.26), channel_id=1, source_target_pairs={{8,0},{12,4},{16,8},{20,12},{24,16},{28,20},{0,24},{4,28},{40,32},... | collective-permute-start | bytes 1572872 | tf_op jit(solution)/shard_map/ppermute | solution.py:31
  160.4 20.4 %collective-permute-start.37 = (bf16[2,256,128]{2,1,0:T(8,128)(2,1)S(1)}, bf16[2,256,128]{2,1,0:T(8,128)(2,1)S(1)}, u32[]{:S(2)}, u32[]{:S(2)}) collective-permute-start(bf16[2,256,128]{2,1,0:T(8,128)(2,1)S(1)} %get-tuple-element.38), channel_id=1, source_target_pairs={{24,0},{28,4},{0,8},{4,12},{8,16},{12,20},{16,24},{20,28},{56,32},... | collective-permute-start | bytes 393224 | tf_op jit(solution)/shard_map/ppermute | solution.py:31
  160.5 21.6 %collective-permute-start.39 = (bf16[2,256,128]{2,1,0:T(8,128)(2,1)S(1)}, bf16[2,256,128]{2,1,0:T(8,128)(2,1)S(1)}, u32[]{:S(2)}, u32[]{:S(2)}) collective-permute-start(bf16[2,256,128]{2,1,0:T(8,128)(2,1)S(1)} %get-tuple-element.39), channel_id=1, source_target_pairs={{8,0},{12,4},{16,8},{20,12},{24,16},{28,20},{0,24},{4,28},{40,32},... | collective-permute-start | bytes 393224 | tf_op jit(solution)/shard_map/ppermute | solution.py:31
  166.7 15.5 %collective-permute-start.38 = (bf16[2,256,128]{2,1,0:T(8,128)(2,1)S(1)}, bf16[2,256,128]{2,1,0:T(8,128)(2,1)S(1)}, u32[]{:S(2)}, u32[]{:S(2)}) collective-permute-start(bf16[2,256,128]{2,1,0:T(8,128)(2,1)S(1)} %get-tuple-element.40), channel_id=1, source_target_pairs={{16,0},{20,4},{24,8},{28,12},{0,16},{4,20},{8,24},{12,28},{48,32},... | collective-permute-start | bytes 393224 | tf_op jit(solution)/shard_map/ppermute | solution.py:31
  176.2 6.8 %collective-permute-start.44 = (bf16[2,256,128]{2,1,0:T(8,128)(2,1)S(1)}, bf16[2,256,128]{2,1,0:T(8,128)(2,1)S(1)}, u32[]{:S(2)}, u32[]{:S(2)}) collective-permute-start(bf16[2,256,128]{2,1,0:T(8,128)(2,1)S(1)} %get-tuple-element.35), channel_id=1, source_target_pairs={{96,0},{100,4},{104,8},{108,12},{112,16},{116,20},{120,24},{124,28... | collective-permute-start | bytes 393224 | tf_op jit(solution)/shard_map/ppermute | solution.py:31
  176.3 6.7 %collective-permute-start.46 = (bf16[2,256,128]{2,1,0:T(8,128)(2,1)S(1)}, bf16[2,256,128]{2,1,0:T(8,128)(2,1)S(1)}, u32[]{:S(2)}, u32[]{:S(2)}) collective-permute-start(bf16[2,256,128]{2,1,0:T(8,128)(2,1)S(1)} %get-tuple-element.36), channel_id=1, source_target_pairs={{32,0},{36,4},{40,8},{44,12},{48,16},{52,20},{56,24},{60,28},{64,3... | collective-permute-start | bytes 393224 | tf_op jit(solution)/shard_map/ppermute | solution.py:31
  180.8 6.5 %collective-permute-start.45 = (bf16[2,256,128]{2,1,0:T(8,128)(2,1)S(1)}, bf16[2,256,128]{2,1,0:T(8,128)(2,1)S(1)}, u32[]{:S(2)}, u32[]{:S(2)}) collective-permute-start(bf16[2,256,128]{2,1,0:T(8,128)(2,1)S(1)} %get-tuple-element.37), channel_id=1, source_target_pairs={{64,0},{68,4},{72,8},{76,12},{80,16},{84,20},{88,24},{92,28},{96,3... | collective-permute-start | bytes 393224 | tf_op jit(solution)/shard_map/ppermute | solution.py:31
  182.3 5.2 %collective-permute-start.40 = (bf16[256,128]{1,0:T(8,128)(2,1)S(1)}, bf16[256,128]{1,0:T(8,128)(2,1)S(1)}, u32[]{:S(2)}, u32[]{:S(2)}) collective-permute-start(bf16[256,128]{1,0:T(8,128)(2,1)S(1)} %get-tuple-element.44), channel_id=1, source_target_pairs={{0,4},{4,0},{8,12},{12,8},{16,20},{20,16},{24,28},{28,24},{32,36},... | collective-permute-start | bytes 196616 | tf_op jit(solution)/shard_map/ppermute | solution.py:39
  187.4 1.3 collective-permute-start.47
  (14 other events, 273.3 us)
